TPU v7x, 32 devices: a whole 2x2x4 slice. The times are simulated.
32 devices in a mesh: group: 2 (over y), expert: 4 (over z), dp: 4 (over x, core).
Axes of the slice: x: 2, y: 2, z: 4, core: 2. Of those that a mesh axis runs over, the one named last changes fastest.
Arguments:
- grad_out: bfloat16 [4096, 2048], P(('group', 'expert', 'dp')), parts along dimension 0, may hold values from -6 to 6
- expert_ids: int32 [4096, 8], P(('group', 'expert', 'dp')), parts along dimension 0, may hold values from 0 to 15, all different within a row; in each aligned block of 128 rows (0 to 127, 128 to 255, ...) at most 128 rows name the same one
- probs: bfloat16 [4096, 8], P(('group', 'expert', 'dp')), parts along dimension 0, may hold values from 0.019897461 to 0.5
- hidden: bfloat16 [4096, 8, 384], P(('group', 'expert', 'dp')), parts along dimension 0, may hold values from -1.5 to 1.5
- weights: bfloat16 [16, 384, 2048], P(('expert', 'dp')), may hold values from -0.125 to 0.125
- momentum: bfloat16 [32, 384, 2048], P(('group', 'expert', 'dp')), parts along dimension 0, may hold values from -6 to 6
Outputs:
- grad_hidden: bfloat16 [4096, 8, 384], P(('group', 'expert', 'dp')), parts along dimension 0
- grad_prob: float32 [4096, 8], P(('group', 'expert', 'dp')), parts along dimension 0
- new_momentum: bfloat16 [32, 384, 2048], P(('group', 'expert', 'dp')), parts along dimension 0
- update: float32 [32, 384, 2048], P(('group', 'expert', 'dp')), parts along dimension 0
There are 2 independent parts, one for each index of `group`. A program takes and returns all parts, laid end to end along the dimension named above; an argument that names none is the same for every part. Nothing has to cross between parts.
Inputs may be any that keep to these rules, and one draw needn't show every extreme that they name: `expert_ids`: each row names 8 different experts; among the 128 rows of one device no expert is named more than 128 times, and in every draw some expert is named exactly 128 times by some device.
All inputs are finite; a program needn't handle non-finite values.
Results may differ from a plain program's by a relative error of at most 0.04.
Values may be sent and summed in bfloat16 or wider, within the bound.
A program may use at most 128 MiB of HBM per device.

v0:
```python
import math

import jax
import jax.numpy as jnp
from jax import lax
from jax.sharding import PartitionSpec as P

EXP_DEV = 4
ITERS = 5


momentum_decay = 0.95
coef_a = 3.4445
coef_b = -4.775
coef_c = 2.0315


def orthogonal(matrix):
    values = matrix.astype(jnp.float32)
    frob_norm = jnp.sqrt(jnp.sum(values * values))
    iterate = (values / (frob_norm + 1e-07)).astype(jnp.bfloat16)
    for step_index in range(ITERS):
        gram_matrix = jnp.dot(iterate, iterate.T, preferred_element_type=jnp.float32).astype(
            jnp.bfloat16
        )
        gram_square = jnp.dot(gram_matrix, gram_matrix, preferred_element_type=jnp.float32)
        poly_mix = (coef_b * gram_matrix.astype(jnp.float32) + coef_c * gram_square).astype(
            jnp.bfloat16
        )
        iterate = (
            coef_a * iterate.astype(jnp.float32)
            + jnp.dot(poly_mix, iterate, preferred_element_type=jnp.float32)
        ).astype(jnp.bfloat16)
    return iterate.astype(jnp.float32) * math.sqrt(matrix.shape[1])


def scale_rows(prob_slots, grad_slots):
    return (prob_slots[..., None].astype(jnp.float32) * grad_slots.astype(jnp.float32)).astype(
        jnp.bfloat16
    )


def shards(grad_out, expert_ids, probs, hidden, weights, momentum):
    tok_rows, model_width = grad_out.shape
    top_count = expert_ids.shape[1]
    hidden_width = hidden.shape[2]
    owner_count = lax.axis_size("expert")
    expert_total = EXP_DEV * owner_count
    capacity = 2 * tok_rows * top_count // expert_total
    routed_rows = tok_rows * top_count
    flat_ids = expert_ids.reshape(-1)
    onehot = (flat_ids[:, None] == jnp.arange(expert_total, dtype=jnp.int32)[None, :]).astype(
        jnp.int32
    )
    before = jnp.cumsum(onehot, 0) - onehot
    position_in = jnp.sum(before * onehot, 1)
    owner_rank = flat_ids // EXP_DEV
    local_index = flat_ids % EXP_DEV
    buffer_index = (local_index * owner_count + owner_rank) * capacity + position_in
    source_map = (
        jnp.zeros((expert_total * capacity,), jnp.int32)
        .at[buffer_index]
        .set(jnp.arange(routed_rows, dtype=jnp.int32) + 1)
    )
    filled = source_map > 0
    source_row = jnp.maximum(source_map - 1, 0)
    hidden_flat = hidden.reshape(routed_rows, hidden_width)
    prob_flat = probs.reshape(-1)
    zero_value = jnp.zeros((), jnp.bfloat16)
    send_grad = jnp.where(filled[:, None], grad_out[source_row // top_count], zero_value).reshape(
        EXP_DEV, owner_count, capacity, model_width
    )
    send_hidden = jnp.where(filled[:, None], hidden_flat[source_row], zero_value).reshape(
        EXP_DEV, owner_count, capacity, hidden_width
    )
    send_prob = jnp.where(filled, prob_flat[source_row], zero_value).reshape(
        EXP_DEV, owner_count, capacity
    )
    recv_grad, recv_hidden, recv_prob = (
        lax.all_to_all(send_grad, "expert", split_axis=1, concat_axis=1, tiled=True),
        lax.all_to_all(send_hidden, "expert", split_axis=1, concat_axis=1, tiled=True),
        lax.all_to_all(send_prob, "expert", split_axis=1, concat_axis=1, tiled=True),
    )
    grad_part = recv_grad
    raw_grad = jnp.einsum(
        "escd,efd->escf",
        grad_part,
        lax.all_gather(weights, "dp", axis=0, tiled=True),
        preferred_element_type=jnp.float32,
    ).astype(jnp.bfloat16)
    grad_part = recv_grad
    scaled = scale_rows(recv_prob, grad_part)
    grad_weights = lax.psum_scatter(
        jnp.einsum(
            "escf,escd->efd", recv_hidden, scaled, preferred_element_type=jnp.float32
        ).astype(jnp.bfloat16),
        "dp",
        scatter_dimension=0,
        tiled=True,
    ).astype(jnp.float32)
    returned = lax.all_to_all(raw_grad, "expert", split_axis=1, concat_axis=1, tiled=True)
    raw_rows = returned.reshape(expert_total * capacity, hidden_width)[buffer_index]
    grad_hidden = (prob_flat[:, None].astype(jnp.float32) * raw_rows.astype(jnp.float32)).astype(
        jnp.bfloat16
    )
    grad_prob = jnp.sum(raw_rows.astype(jnp.float32) * hidden_flat.astype(jnp.float32), 1)
    new_momentum = (momentum_decay * momentum.astype(jnp.float32) + grad_weights).astype(
        jnp.bfloat16
    )
    update = jax.vmap(orthogonal)(new_momentum)
    return (
        grad_hidden.reshape(tok_rows, top_count, hidden_width),
        grad_prob.reshape(tok_rows, top_count),
        new_momentum,
        update,
    )


def solution(mesh):
    in_specs = (
        P(("group", "expert", "dp"), None),
        P(("group", "expert", "dp"), None),
        P(("group", "expert", "dp"), None),
        P(("group", "expert", "dp"), None, None),
        P(("expert", "dp"), None, None),
        P(("group", "expert", "dp"), None, None),
    )
    out_specs = (
        P(("group", "expert", "dp"), None, None),
        P(("group", "expert", "dp"), None),
        P(("group", "expert", "dp"), None, None),
        P(("group", "expert", "dp"), None, None),
    )
    return jax.shard_map(shards, mesh=mesh, in_specs=in_specs, out_specs=out_specs, check_vma=False)
```

profile of v0, /device:TPU:15, one launch (start us, length us, event | category | flops | bytes accessed | tf_op | source)
XLA Modules:
  0.0 381.9 jit_solution(17192612257264533717)
XLA Ops:
  8.4 4.5 %reduce-window.6 = s32[16,8,128]{2,1,0:T(8,128)S(1)} reduce-window(s32[16,8,128]{2,1,0:T(8,128)S(1)} %fusion.82, s32[]{:T(128)} %constant.60.clone.1), window={size=1x1x128 pad=0_0x0_0x127_0}, to_apply=%region_0.0 | reduce-window | flops 2080768 | bytes 131076 | tf_op jit(solution)/shard_map/reduce-window
  13.4 4.3 %scatter_custom_fusion = s32[2048]{0:T(1024)S(1)} fusion(s32[1024]{0:T(1024)S(1)} %bitcast.116, s32[1024]{0:T(1024)S(1)} %iota_add_fusion, s32[]{:T(128)} %constant.60.clone.1), kind=kCustom, calls=%fused_computation.116 | custom fusion | bytes 8196 | tf_op jit(solution)/shard_map/scatter | solution.py:63
  18.7 13.1 %gather_fusion.3 = bf16[2048]{0:T(1024)(128)(2,1)S(1)} fusion(bf16[1024]{0:T(1024)(128)(2,1)S(1)} %reshape.307, s32[2048]{0:T(1024)S(1)} %get-tuple-element.18), kind=kCustom, calls=%fused_computation.3 | custom fusion | bytes 16384 | tf_op jit(solution)/shard_map/gather | solution.py:76
  32.4 4.8 %all-to-all-start.3 = ((bf16[4,4,128]{2,0,1:T(4,128)(2,1)}), bf16[4,4,128]{2,0,1:T(4,128)(2,1)S(1)}, u32[]{:S(2)}, u32[]{:S(2)}) async-start(bf16[4,4,128]{2,0,1:T(4,128)(2,1)} %copy.50), calls=%async_computation.3 | async-start | bytes 8192 | tf_op jit(solution)/shard_map/all_to_all | solution.py:82
  37.1 7.4 %gather_fusion.2 = bf16[2048,384]{1,0:T(8,128)(2,1)S(1)} fusion(bf16[1024,384]{1,0:T(8,128)(2,1)S(1)} %bitcast.107, s32[2048]{0:T(1024)S(1)} %get-tuple-element.18), kind=kCustom, calls=%fused_computation.2 | custom fusion | bytes 3153920 | tf_op jit(solution)/shard_map/gather | solution.py:73
  45.9 2.6 copy.48
  48.5 4.5 %all-to-all-start.2 = ((bf16[4,4,128,384]{2,3,0,1:T(8,128)(2,1)}), bf16[4,4,128,384]{2,3,0,1:T(8,128)(2,1)S(1)}, u32[]{:S(2)}, u32[]{:S(2)}) async-start(bf16[4,4,128,384]{2,3,0,1:T(8,128)(2,1)} %copy.48), calls=%async_computation.2 | async-start | bytes 3145728 | tf_op jit(solution)/shard_map/all_to_all | solution.py:81
  53.1 11.0 %gather_fusion = bf16[2048,2048]{1,0:T(8,128)(2,1)} fusion(bf16[128,2048]{1,0:T(8,128)(2,1)S(1)} %copy-done, s32[2048]{0:T(1024)S(1)} %get-tuple-element.19), kind=kCustom, calls=%fused_computation | custom fusion | bytes 16785408 | tf_op jit(solution)/shard_map/gather | solution.py:70
  64.0 7.2 %copy_select_fusion = bf16[4,4,128,2048]{3,2,0,1:T(8,128)(2,1)} fusion(bf16[4,4,128,2048]{3,2,1,0:T(8,128)(2,1)} %bitcast.109, pred[4,4,128]{2,0,1:T(4,128)(4,1)S(1)} %copy.43), kind=kLoop, calls=%fused_computation.10 | loop fusion | flops 4194304 | bytes 16779264 | tf_op jit(solution)/shard_map/jit(_where)/select_n | solution.py:70
  71.2 14.3 %all-to-all-done.2 = bf16[4,4,128,384]{2,3,0,1:T(8,128)(2,1)S(1)} async-done(((bf16[4,4,128,384]{2,3,0,1:T(8,128)(2,1)}), bf16[4,4,128,384]{2,3,0,1:T(8,128)(2,1)S(1)}, u32[]{:S(2)}, u32[]{:S(2)}) %all-to-all-start.2) | async-done | bytes 1572896 | tf_op jit(solution)/shard_map/all_to_all | solution.py:81
  85.5 9.6 %all-to-all-start = ((bf16[4,4,128,2048]{3,2,0,1:T(8,128)(2,1)}), bf16[4,4,128,2048]{3,2,0,1:T(8,128)(2,1)}, u32[]{:S(2)}, u32[]{:S(2)}) async-start(bf16[4,4,128,2048]{3,2,0,1:T(8,128)(2,1)} %copy_select_fusion), calls=%async_computation | async-start | bytes 16777216 | tf_op jit(solution)/shard_map/all_to_all | solution.py:80
  95.9 177.8 %all-to-all-done = bf16[4,4,128,2048]{3,2,0,1:T(8,128)(2,1)} async-done(((bf16[4,4,128,2048]{3,2,0,1:T(8,128)(2,1)}), bf16[4,4,128,2048]{3,2,0,1:T(8,128)(2,1)}, u32[]{:S(2)}, u32[]{:S(2)}) %all-to-all-start) | async-done | bytes 8388640 | tf_op jit(solution)/shard_map/all_to_all | solution.py:80
  273.7 8.9 %bitcast_convert_fusion = bf16[4,384,2048]{2,1,0:T(8,128)(2,1)} fusion(bf16[4,4,128,384]{2,3,0,1:T(8,128)(2,1)S(1)} %all-to-all-done.2, bf16[4,4,128,2048]{3,2,0,1:T(8,128)(2,1)} %all-to-all-done, f32[4,4,128]{2,0,1:T(4,128)S(1)} %convert_element_type.165), kind=kOutput, calls=%fused_computation.6 | convolution fusion | flops 3236954112 | bytes 16261120 | tf_op jit(solution)/shard_map/escf,escd->efd/dot_general | solution.py:94
  282.7 9.7 %fusion.12 = bf16[4,4,128,384]{3,2,1,0:T(8,128)(2,1)S(1)} fusion(bf16[4,384,2048]{2,1,0:T(8,128)(2,1)} %all-gather.2.cloned.1.call-done, bf16[4,4,128,2048]{3,2,0,1:T(8,128)(2,1)} %all-to-all-done), kind=kOutput, calls=%fused_computation.31 | convolution fusion | flops 3222011904 | bytes 16252928 | tf_op jit(solution)/shard_map/escd,efd->escf/dot_general | solution.py:85
  293.7 8.4 %all-to-all-start.1 = ((bf16[4,4,128,384]{3,2,0,1:T(8,128)(2,1)}), bf16[4,4,128,384]{3,2,0,1:T(8,128)(2,1)}, u32[]{:S(2)}, u32[]{:S(2)}) async-start(bf16[4,4,128,384]{3,2,0,1:T(8,128)(2,1)} %copy.46), calls=%async_computation.1 | async-start | bytes 3145728 | tf_op jit(solution)/shard_map/all_to_all | solution.py:101
  302.2 32.1 %all-to-all-done.1 = bf16[4,4,128,384]{3,2,0,1:T(8,128)(2,1)} async-done(((bf16[4,4,128,384]{3,2,0,1:T(8,128)(2,1)}), bf16[4,4,128,384]{3,2,0,1:T(8,128)(2,1)}, u32[]{:S(2)}, u32[]{:S(2)}) %all-to-all-start.1) | async-done | bytes 1572896 | tf_op jit(solution)/shard_map/all_to_all | solution.py:101
  336.0 5.0 %gather_fusion.1 = bf16[1024,384]{1,0:T(8,128)(2,1)} fusion(bf16[2048,384]{1,0:T(8,128)(2,1)S(1)} %bitcast.108, s32[1024]{0:T(1024)S(1)} %broadcast_clamp_fusion), kind=kCustom, calls=%fused_computation.1 | custom fusion | bytes 1576960 | tf_op jit(solution)/shard_map/gather | solution.py:102
  344.2 3.9 %fusion.5 = (f32[]{:T(128)}, bf16[1,384,2048]{2,1,0:T(8,128)(2,1)}) fusion(bf16[1,384,2048]{2,1,0:T(8,128)(2,1)} %reduce-scatter.2.cloned.1.call-done, bf16[1,384,2048]{2,1,0:T(8,128)(2,1)S(1)} %copy-done.3), kind=kLoop, calls=%fused_computation.15 | loop fusion | flops 6291455 | bytes 4718596 | tf_op jit(solution)/shard_map/vmap()/reduce_sum | solution.py:20
  348.9 3.1 fusion.44
  354.4 3.0 fusion.47
  359.8 3.0 fusion.50
  365.2 2.9 fusion.53
  368.0 3.1 fusion.8
  372.2 2.9 convert_multiply_fusion.1
  (55 shorter events, 19.9 us)
Async XLA Ops:
  7.2 45.9 %copy-start = (bf16[128,2048]{1,0:T(8,128)(2,1)S(1)}, bf16[128,2048]{1,0:T(8,128)(2,1)}, u32[]{:S(2)}) copy-start(bf16[128,2048]{1,0:T(8,128)(2,1)} %param.6) | copy-start | bytes 1572868
  7.2 29.9 %copy-start.2 = (bf16[128,8,384]{2,1,0:T(8,128)(2,1)S(1)}, bf16[128,8,384]{2,1,0:T(8,128)(2,1)}, u32[]{:S(2)}) copy-start(bf16[128,8,384]{2,1,0:T(8,128)(2,1)} %param.9) | copy-start | bytes 2359300
  32.4 16.2 %all-to-all-start.3 = ((bf16[4,4,128]{2,0,1:T(4,128)(2,1)}), bf16[4,4,128]{2,0,1:T(4,128)(2,1)S(1)}, u32[]{:S(2)}, u32[]{:S(2)}) async-start(bf16[4,4,128]{2,0,1:T(4,128)(2,1)} %copy.50), calls=%async_computation.3 | async-start | bytes 8192 | tf_op jit(solution)/shard_map/all_to_all | solution.py:82
  48.5 37.0 %all-to-all-start.2 = ((bf16[4,4,128,384]{2,3,0,1:T(8,128)(2,1)}), bf16[4,4,128,384]{2,3,0,1:T(8,128)(2,1)S(1)}, u32[]{:S(2)}, u32[]{:S(2)}) async-start(bf16[4,4,128,384]{2,3,0,1:T(8,128)(2,1)} %copy.48), calls=%async_computation.2 | async-start | bytes 3145728 | tf_op jit(solution)/shard_map/all_to_all | solution.py:81
  85.5 188.2 %all-to-all-start = ((bf16[4,4,128,2048]{3,2,0,1:T(8,128)(2,1)}), bf16[4,4,128,2048]{3,2,0,1:T(8,128)(2,1)}, u32[]{:S(2)}, u32[]{:S(2)}) async-start(bf16[4,4,128,2048]{3,2,0,1:T(8,128)(2,1)} %copy_select_fusion), calls=%async_computation | async-start | bytes 16777216 | tf_op jit(solution)/shard_map/all_to_all | solution.py:80
  95.1 187.6 %all-gather.2.cloned.1.call-start = ((), (), s32[]{:S(2)}) async-start(), calls=%async_computation.5 | async-start | bytes 7864320 | tf_op jit(solution)/shard_map/all_gather | solution.py:88
  95.8 248.4 %reduce-scatter.2.cloned.1.call-start = ((), (), s32[]{:S(2)}) async-start(), calls=%async_computation.6 | async-start | bytes 7864320 | tf_op jit(solution)/shard_map/reduce_scatter | solution.py:93
  292.4 9.7 %copy-start.5 = (bf16[128,8]{0,1:T(8,128)(2,1)S(1)}, bf16[128,8]{0,1:T(8,128)(2,1)}, u32[]{:S(2)}) copy-start(bf16[128,8]{0,1:T(8,128)(2,1)} %param.8) | copy-start | bytes 6148
  293.7 40.6 %all-to-all-start.1 = ((bf16[4,4,128,384]{3,2,0,1:T(8,128)(2,1)}), bf16[4,4,128,384]{3,2,0,1:T(8,128)(2,1)}, u32[]{:S(2)}, u32[]{:S(2)}) async-start(bf16[4,4,128,384]{3,2,0,1:T(8,128)(2,1)} %copy.46), calls=%async_computation.1 | async-start | bytes 3145728 | tf_op jit(solution)/shard_map/all_to_all | solution.py:101
  341.0 3.2 copy-start.3
  348.8 3.1 copy-start.4
  354.4 3.0 copy-start.6
  359.8 3.0 copy-start.7
  371.2 3.9 %copy-start.1 = (bf16[128,2048]{1,0:T(8,128)(2,1)S(1)}, bf16[128,2048]{1,0:T(8,128)(2,1)}, u32[]{:S(2)}) copy-start(bf16[128,2048]{1,0:T(8,128)(2,1)} %param.6) | copy-start | bytes 1572868
Sparse Core Ops, SparseCore 0:
  97.5 47.8 all-gather.1
  282.8 61.0 reduce-scatter.1
where the time goes:
time: 389 us; the launch traced here: 382 us
  waiting for transfers between devices  225 us (58%)
  local copies, waits for them, and re-layouts  50.2 us (13%)
  matrix products  44.7 us (11%)
  starting transfers between devices  27.3 us (7%)
  other arithmetic  19.8 us (5%)
  between operations  15 us (4%)
    all_to_all x1, waiting for transfers between devices, shards(): lax.all_to_all(send_grad, 'expert', split_axis=1, concat_axis=1, tiled=True)  178 us
    all_to_all x1, waiting for transfers between devices, shards(): lax.all_to_all(raw_grad, 'expert', split_axis=1, concat_axis=1, tiled=True)  32.1 us
    all_to_all x1, waiting for transfers between devices, shards(): lax.all_to_all(send_hidden, 'expert', split_axis=1, concat_axis=1, tiled=...  14.3 us
    dot_general x5, matrix products, orthogonal(): jnp.dot(poly_mix, iterate, preferred_element_type=jnp.float32)  13.2 us
    gather x1, local copies, waits for them, and re-layouts, shards(): prob_flat[source_row]  13.1 us
    dot_general x5, matrix products, orthogonal(): jnp.dot(iterate, iterate.T, preferred_element_type=jnp.float32)  13 us
    gather x1, local copies, waits for them, and re-layouts, shards(): grad_out[source_row // top_count]  11 us
    dot_general x1, matrix products, shards(): jnp.einsum('escd,efd->escf', grad_part, lax.all_gather(weights, 'dp', axi...  9.66 us
  transfers between devices with their start and end apart: 6, of which 3 were waited for; matrix products, arithmetic and copies ran while one was open for 16% of the time, Pallas kernels for 0%

commit v1 on v0

--- a/solution.py
+++ b/solution.py
@@ -116,6 +116,55 @@
     )
 
 
+def dense_shards(grad_out, expert_ids, probs, hidden, weights, momentum):
+    axes = ("expert", "dp")
+    tok_rows, model_width = grad_out.shape
+    top_count = expert_ids.shape[1]
+    hidden_width = hidden.shape[2]
+    device_count = lax.axis_size("expert") * lax.axis_size("dp")
+    expert_total = device_count * weights.shape[0]
+    all_grad = lax.all_gather(grad_out, axes, axis=0, tiled=True)
+    experts = jnp.arange(expert_total, dtype=jnp.int32)
+    zero_value = jnp.zeros((), jnp.bfloat16)
+    prob_hidden = (probs[..., None].astype(jnp.float32) * hidden.astype(jnp.float32)).astype(
+        jnp.bfloat16
+    )
+    send_hidden = jnp.zeros((expert_total, tok_rows, hidden_width), jnp.bfloat16)
+    for choice in range(top_count):
+        named = expert_ids[None, :, choice] == experts[:, None]
+        send_hidden = jnp.where(named[..., None], prob_hidden[None, :, choice], send_hidden)
+    recv_hidden = lax.all_to_all(send_hidden, axes, split_axis=0, concat_axis=0, tiled=True)
+    raw_grad = lax.dot_general(
+        all_grad, weights[0], (((1,), (1,)), ((), ())), preferred_element_type=jnp.float32
+    ).astype(jnp.bfloat16)
+    returned = lax.all_to_all(
+        raw_grad.reshape(device_count, tok_rows, hidden_width),
+        axes,
+        split_axis=0,
+        concat_axis=0,
+        tiled=True,
+    )
+    grad_weights = lax.dot_general(
+        recv_hidden.reshape(device_count * tok_rows, hidden_width),
+        all_grad,
+        (((0,), (0,)), ((), ())),
+        preferred_element_type=jnp.float32,
+    )[None]
+    new_momentum = (momentum_decay * momentum.astype(jnp.float32) + grad_weights).astype(
+        jnp.bfloat16
+    )
+    update = jax.vmap(orthogonal)(new_momentum)
+    raw_rows = jnp.zeros((tok_rows, top_count, hidden_width), jnp.bfloat16)
+    for expert in range(expert_total):
+        named = expert_ids == expert
+        raw_rows = jnp.where(named[..., None], returned[expert][:, None], raw_rows)
+    grad_hidden = (probs[..., None].astype(jnp.float32) * raw_rows.astype(jnp.float32)).astype(
+        jnp.bfloat16
+    )
+    grad_prob = jnp.sum(raw_rows.astype(jnp.float32) * hidden.astype(jnp.float32), 2)
+    return grad_hidden, grad_prob, new_momentum, update
+
+
 def solution(mesh):
     in_specs = (
         P(("group", "expert", "dp"), None),
@@ -131,4 +180,22 @@
         P(("group", "expert", "dp"), None, None),
         P(("group", "expert", "dp"), None, None),
     )
-    return jax.shard_map(shards, mesh=mesh, in_specs=in_specs, out_specs=out_specs, check_vma=False)
+
+    owners = mesh.shape["expert"]
+    dp_count = mesh.shape["dp"]
+
+    def program(grad_out, expert_ids, probs, hidden, weights, momentum):
+        tok_rows = grad_out.shape[0] // (mesh.shape["group"] * owners * dp_count)
+        expert_total = weights.shape[0]
+        dense = expert_total == owners * dp_count and (
+            2 * tok_rows * expert_ids.shape[1] // expert_total >= tok_rows
+        )
+        return jax.shard_map(
+            dense_shards if dense else shards,
+            mesh=mesh,
+            in_specs=in_specs,
+            out_specs=out_specs,
+            check_vma=False,
+        )(grad_out, expert_ids, probs, hidden, weights, momentum)
+
+    return program

time: 389 us -> 228 us (0.59); the launches traced: 382 us -> 227 us
  waiting for transfers between devices: 225 us -> 149 us
  local copies, waits for them, and re-layouts: 50.2 us -> 2.58 us
  starting transfers between devices: 27.3 us -> 10.5 us
  other arithmetic: 19.8 us -> 7.97 us
    all_to_all x4 -> x2, waiting for transfers between devices: 224 us -> 71 us  [the longest x1 36.1 us: dense_shards(): lax.all_to_all(raw_grad.reshape(device_count, tok_rows, hidden_width), ax...]
    all_gather x1, waiting for transfers between devices: 0.02 us -> 77.2 us  [dense_shards(): all_grad = lax.all_gather(grad_out, axes, axis=0, tiled=True)]
    gather x4 -> x0, local copies, waits for them, and re-layouts: 36.5 us -> none  [the longest x1 13.1 us: shards(): prob_flat[source_row]]
    all_to_all x4 -> x2, starting transfers between devices: 27.2 us -> 10.5 us  [the longest x1 5.6 us: dense_shards(): lax.all_to_all(raw_grad.reshape(device_count, tok_rows, hidden_width), ax...]
    another operation x3 -> x0, other arithmetic: 4.64 us -> none
    scatter x1 -> x0, local copies, waits for them, and re-layouts: 4.32 us -> none  [shards(): source_map = jnp.zeros((expert_total * capacity,), jnp.int32).at[buffer_i...]
    select_n x4 -> x1, other arithmetic: 8.59 us -> 4.48 us  [dense_shards(): jnp.where(named[..., None], prob_hidden[None, :, choice], send_hidden)]
  transfers between devices with their start and end apart: 6 -> 3, of which waited for: 3 -> 3; matrix products, arithmetic and copies ran while one was open for 16% -> 1% of each run, Pallas kernels for 0% -> 0%
where the time goes in v1:
time: 228 us; the launch traced here: 227 us
  waiting for transfers between devices  149 us (65%)
  matrix products  42.6 us (19%)
  between operations  14.9 us (7%)
  starting transfers between devices  10.5 us (5%)
  other arithmetic  7.97 us (3%)
  local copies, waits for them, and re-layouts  2.58 us (1%)
    all_gather x1, waiting for transfers between devices, dense_shards(): all_grad = lax.all_gather(grad_out, axes, axis=0, tiled=True)  77.2 us
    all_to_all x1, waiting for transfers between devices, dense_shards(): lax.all_to_all(raw_grad.reshape(device_count, tok_rows, hidden_width), ax...  36.1 us
    all_to_all x1, waiting for transfers between devices, dense_shards(): lax.all_to_all(send_hidden, axes, split_axis=0, concat_axis=0, tiled=True)  34.9 us
    dot_general x5, matrix products, orthogonal(): jnp.dot(poly_mix, iterate, preferred_element_type=jnp.float32)  13.3 us
    dot_general x5, matrix products, orthogonal(): jnp.dot(iterate, iterate.T, preferred_element_type=jnp.float32)  11.3 us
    dot_general x1, matrix products, dense_shards(): lax.dot_general(all_grad, weights[0], (((1,), (1,)), ((), ())), preferred...  9.07 us
    dot_general x1, matrix products, dense_shards(): lax.dot_general(recv_hidden.reshape(device_count * tok_rows, hidden_width...  8.89 us
    all_to_all x1, starting transfers between devices, dense_shards(): lax.all_to_all(raw_grad.reshape(device_count, tok_rows, hidden_width), ax...  5.6 us
  transfers between devices with their start and end apart: 3, of which 3 were waited for; matrix products, arithmetic and copies ran while one was open for 1% of the time, Pallas kernels for 0%

profile of v1, /device:TPU:15, one launch (start us, length us, event | category | flops | bytes accessed | tf_op | source)
XLA Modules:
  0.0 227.5 jit_solution(2783274859189834807)
XLA Ops:
  7.2 0.7 all-gather.2.cloned.1.call-update
  7.9 77.2 %all-gather.2.cloned.1.call-done = bf16[2048,2048]{1,0:T(8,128)(2,1)} async-done(((bf16[128,2048]{1,0:T(8,128)(2,1)}), bf16[2048,2048]{1,0:T(8,128)(2,1)}) %all-gather.2.cloned.1.call-update) | async-done | bytes 8388624 | tf_op jit(solution)/shard_map/all_gather | solution.py:126
  85.1 9.1 %convolution_convert_fusion = bf16[2048,384]{1,0:T(8,128)(2,1)} fusion(bf16[2048,2048]{1,0:T(8,128)(2,1)} %all-gather.2.cloned.1.call-done, bf16[1,384,2048]{2,1,0:T(8,128)(2,1)S(1)} %copy-done), kind=kOutput, calls=%fused_computation.17 | convolution fusion | flops 3222011904 | bytes 11534336 | tf_op jit(solution)/shard_map/dot_general | solution.py:137
  94.2 5.6 %all-to-all-start = ((bf16[16,128,384]{2,1,0:T(8,128)(2,1)}), bf16[16,128,384]{2,1,0:T(8,128)(2,1)S(1)}, u32[]{:S(2)}, u32[]{:S(2)}) async-start(bf16[16,128,384]{2,1,0:T(8,128)(2,1)} %bitcast.143), calls=%async_computation | async-start | bytes 3145728 | tf_op jit(solution)/shard_map/all_to_all | solution.py:140
  99.9 36.1 %all-to-all-done = bf16[16,128,384]{2,1,0:T(8,128)(2,1)S(1)} async-done(((bf16[16,128,384]{2,1,0:T(8,128)(2,1)}), bf16[16,128,384]{2,1,0:T(8,128)(2,1)S(1)}, u32[]{:S(2)}, u32[]{:S(2)}) %all-to-all-start) | async-done | bytes 1572896 | tf_op jit(solution)/shard_map/all_to_all | solution.py:140
  136.0 0.2 slice_bitcast_fusion.23
  136.2 0.9 copy-done.1
  137.1 3.1 %fusion.9 = (f32[128,8]{0,1:T(8,128)}, bf16[128,8,384]{2,0,1:T(8,128)(2,1)S(1)}) fusion(bf16[128,8,384]{2,1,0:T(8,128)(2,1)S(1)} %copy-done.1, bf16[128,384]{1,0:T(8,128)(2,1)S(1)} %get-tuple-element.11, pred[128,8]{0,1:T(8,128)(4,1)S(1)} %get-tuple-element.45, bf16[128,384]{1,0:T(8,128)(2,1)S(1)} %get-tuple-element.12, ...), kind=kLoop, calls=%fused_computation.22 | loop fusion | flops 7863296 | bytes 3166208 | tf_op jit(solution)/shard_map/reduce_sum | solution.py:164
  140.2 0.3 fusion.10
  140.7 4.5 %select_select_fusion = bf16[16,128,384]{2,1,0:T(8,128)(2,1)} fusion(pred[16,128]{1,0:T(8,128)(4,1)S(1)} %get-tuple-element.62, pred[16,128]{1,0:T(8,128)(4,1)S(1)} %get-tuple-element.63, pred[16,128]{1,0:T(8,128)(4,1)S(1)} %get-tuple-element.64, pred[16,128]{1,0:T(8,128)(4,1)S(1)} %get-tuple-element.65, pred[16,128]{1,0:T(8,128)(4,1)S(1)} %get-tuple-element.66, ...), kind=kLoop, calls=%fused_computation.40 | loop fusion | flops 6291456 | bytes 2375680 | tf_op jit(solution)/shard_map/jit(_where)/select_n | solution.py:135
  145.1 4.9 %all-to-all-start.1 = ((bf16[16,128,384]{2,1,0:T(8,128)(2,1)}), bf16[16,128,384]{2,1,0:T(8,128)(2,1)}, u32[]{:S(2)}, u32[]{:S(2)}) async-start(bf16[16,128,384]{2,1,0:T(8,128)(2,1)} %select_select_fusion), calls=%async_computation.1 | async-start | bytes 3145728 | tf_op jit(solution)/shard_map/all_to_all | solution.py:136
  150.0 1.3 copy.28
  151.4 34.9 %all-to-all-done.1 = bf16[16,128,384]{2,1,0:T(8,128)(2,1)} async-done(((bf16[16,128,384]{2,1,0:T(8,128)(2,1)}), bf16[16,128,384]{2,1,0:T(8,128)(2,1)}, u32[]{:S(2)}, u32[]{:S(2)}) %all-to-all-start.1) | async-done | bytes 1572896 | tf_op jit(solution)/shard_map/all_to_all | solution.py:136
  186.3 8.9 %fusion = (f32[]{:T(128)}, bf16[1,384,2048]{2,1,0:T(8,128)(2,1)S(1)}) fusion(bf16[2048,384]{1,0:T(8,128)(2,1)} %bitcast.34, bf16[2048,2048]{1,0:T(8,128)(2,1)} %all-gather.2.cloned.1.call-done, bf16[1,384,2048]{2,1,0:T(8,128)(2,1)} %param.11), kind=kOutput, calls=%fused_computation.2 | convolution fusion | flops 3226730496 | bytes 13107204 | tf_op jit(solution)/shard_map/dot_general | solution.py:147
  195.9 1.0 fusion.37
  196.9 2.4 %fusion.6 = bf16[1,384,2048]{2,1,0:T(8,128)(2,1)} fusion(bf16[384,384]{1,0:T(8,128)(2,1)S(1)} %fusion.37, f32[]{:T(128)S(6)} %add.43, bf16[1,384,2048]{2,1,0:T(8,128)(2,1)S(1)} %get-tuple-element.61), kind=kOutput, calls=%fused_computation.13 | convolution fusion | flops 725827584 | bytes 3440644 | tf_op jit(solution)/shard_map/vmap()/dot_general | solution.py:32
  199.4 3.2 %fusion.40 = bf16[384,384]{1,0:T(8,128)(2,1)S(1)} fusion(bf16[1,384,2048]{2,1,0:T(8,128)(2,1)} %fusion.6), kind=kOutput, calls=%fused_computation.57 | convolution fusion | flops 604127232 | bytes 1867776 | tf_op jit(solution)/shard_map/vmap()/dot_general | solution.py:23
  202.5 2.4 %fusion.5 = bf16[1,384,2048]{2,1,0:T(8,128)(2,1)} fusion(bf16[1,384,2048]{2,1,0:T(8,128)(2,1)S(1)} %copy-done.5, bf16[384,384]{1,0:T(8,128)(2,1)S(1)} %fusion.40), kind=kOutput, calls=%fused_computation.11 | convolution fusion | flops 721108992 | bytes 3440640 | tf_op jit(solution)/shard_map/vmap()/dot_general | solution.py:32
  204.9 3.2 %fusion.43 = bf16[384,384]{1,0:T(8,128)(2,1)S(1)} fusion(bf16[1,384,2048]{2,1,0:T(8,128)(2,1)} %fusion.5), kind=kOutput, calls=%fused_computation.58 | convolution fusion | flops 604127232 | bytes 1867776 | tf_op jit(solution)/shard_map/vmap()/dot_general | solution.py:23
  208.1 2.4 %fusion.4 = bf16[1,384,2048]{2,1,0:T(8,128)(2,1)} fusion(bf16[1,384,2048]{2,1,0:T(8,128)(2,1)S(1)} %copy-done.6, bf16[384,384]{1,0:T(8,128)(2,1)S(1)} %fusion.43), kind=kOutput, calls=%fused_computation.9 | convolution fusion | flops 721108992 | bytes 3440640 | tf_op jit(solution)/shard_map/vmap()/dot_general | solution.py:32
  210.5 3.0 %fusion.46 = bf16[384,384]{1,0:T(8,128)(2,1)S(1)} fusion(bf16[1,384,2048]{2,1,0:T(8,128)(2,1)} %fusion.4), kind=kOutput, calls=%fused_computation.59 | convolution fusion | flops 604127232 | bytes 1867776 | tf_op jit(solution)/shard_map/vmap()/dot_general | solution.py:23
  213.5 3.2 %fusion.3 = bf16[1,384,2048]{2,1,0:T(8,128)(2,1)S(1)} fusion(bf16[1,384,2048]{2,1,0:T(8,128)(2,1)} %fusion.4, bf16[384,384]{1,0:T(8,128)(2,1)S(1)} %fusion.46), kind=kOutput, calls=%fused_computation.7 | convolution fusion | flops 721108992 | bytes 3440640 | tf_op jit(solution)/shard_map/vmap()/dot_general | solution.py:32
  216.7 1.0 fusion.49
  217.7 2.9 %convert_multiply_fusion.1 = f32[1,384,2048]{2,1,0:T(8,128)} fusion(bf16[1,384,2048]{2,1,0:T(8,128)(2,1)S(1)} %fusion.3, bf16[384,384]{1,0:T(8,128)(2,1)S(1)} %fusion.49), kind=kOutput, calls=%fused_computation.16 | convolution fusion | flops 722681856 | bytes 5013504 | tf_op jit(solution)/shard_map/vmap()/dot_general | solution.py:32
  (22 shorter events, 0.2 us)
Async XLA Ops:
  7.2 78.0 %copy-start = (bf16[1,384,2048]{2,1,0:T(8,128)(2,1)S(1)}, bf16[1,384,2048]{2,1,0:T(8,128)(2,1)}, u32[]{:S(2)}) copy-start(bf16[1,384,2048]{2,1,0:T(8,128)(2,1)} %param.10) | copy-start | bytes 4718596
  7.2 77.9 %all-gather.2.cloned.1.call-start = ((), (), s32[]{:S(2)}) async-start(), calls=%async_computation.2 | async-start | bytes 8912896 | tf_op jit(solution)/shard_map/all_gather | solution.py:126
  94.2 5.6 %copy-start.3 = (bf16[128,8]{0,1:T(8,128)(2,1)S(1)}, bf16[128,8]{0,1:T(8,128)(2,1)}, u32[]{:S(2)}) copy-start(bf16[128,8]{0,1:T(8,128)(2,1)} %param.8) | copy-start | bytes 6148
  94.2 5.6 %copy-start.2 = (s32[128,8]{0,1:T(8,128)S(1)}, s32[128,8]{0,1:T(8,128)}, u32[]{:S(2)}) copy-start(s32[128,8]{0,1:T(8,128)} %param.7) | copy-start | bytes 12292
  94.2 41.8 %all-to-all-start = ((bf16[16,128,384]{2,1,0:T(8,128)(2,1)}), bf16[16,128,384]{2,1,0:T(8,128)(2,1)S(1)}, u32[]{:S(2)}, u32[]{:S(2)}) async-start(bf16[16,128,384]{2,1,0:T(8,128)(2,1)} %bitcast.143), calls=%async_computation | async-start | bytes 3145728 | tf_op jit(solution)/shard_map/all_to_all | solution.py:140
  136.0 1.1 copy-start.1
  145.1 41.2 %all-to-all-start.1 = ((bf16[16,128,384]{2,1,0:T(8,128)(2,1)}), bf16[16,128,384]{2,1,0:T(8,128)(2,1)}, u32[]{:S(2)}, u32[]{:S(2)}) async-start(bf16[16,128,384]{2,1,0:T(8,128)(2,1)} %select_select_fusion), calls=%async_computation.1 | async-start | bytes 3145728 | tf_op jit(solution)/shard_map/all_to_all | solution.py:136
  195.2 1.7 copy-start.4
  199.4 3.2 %copy-start.5 = (bf16[1,384,2048]{2,1,0:T(8,128)(2,1)S(1)}, bf16[1,384,2048]{2,1,0:T(8,128)(2,1)}, u32[]{:S(2)}) copy-start(bf16[1,384,2048]{2,1,0:T(8,128)(2,1)} %fusion.6) | copy-start | bytes 4718596
  204.9 3.2 %copy-start.6 = (bf16[1,384,2048]{2,1,0:T(8,128)(2,1)S(1)}, bf16[1,384,2048]{2,1,0:T(8,128)(2,1)}, u32[]{:S(2)}) copy-start(bf16[1,384,2048]{2,1,0:T(8,128)(2,1)} %fusion.5) | copy-start | bytes 4718596
Sparse Core Ops, SparseCore 0:
  10.2 74.8 all-gather.1

commit v2 on v1

--- a/solution.py
+++ b/solution.py
@@ -134,9 +134,11 @@
         named = expert_ids[None, :, choice] == experts[:, None]
         send_hidden = jnp.where(named[..., None], prob_hidden[None, :, choice], send_hidden)
     recv_hidden = lax.all_to_all(send_hidden, axes, split_axis=0, concat_axis=0, tiled=True)
+    all_grad, recv_hidden = lax.optimization_barrier((all_grad, recv_hidden))
     raw_grad = lax.dot_general(
         all_grad, weights[0], (((1,), (1,)), ((), ())), preferred_element_type=jnp.float32
     ).astype(jnp.bfloat16)
+    raw_grad, recv_hidden = lax.optimization_barrier((raw_grad, recv_hidden))
     returned = lax.all_to_all(
         raw_grad.reshape(device_count, tok_rows, hidden_width),
         axes,
@@ -154,6 +156,7 @@
         jnp.bfloat16
     )
     update = jax.vmap(orthogonal)(new_momentum)
+    update, returned = lax.optimization_barrier((update, returned))
     raw_rows = jnp.zeros((tok_rows, top_count, hidden_width), jnp.bfloat16)
     for expert in range(expert_total):
         named = expert_ids == expert

time: 228 us -> 183 us (0.80)
  waiting for transfers between devices: 149 us -> 89.3 us
  matrix products: 42.6 us -> 52.2 us
    all_gather x1, waiting for transfers between devices: 77.2 us -> 32.9 us  [dense_shards(): all_grad = lax.all_gather(grad_out, axes, axis=0, tiled=True)]
    all_to_all x1, waiting for transfers between devices: 36.1 us -> 0.01 us  [dense_shards(): lax.all_to_all(raw_grad.reshape(device_count, tok_rows, hidden_width), ax...]
    all_to_all x1, waiting for transfers between devices: 34.9 us -> 55.8 us  [dense_shards(): lax.all_to_all(send_hidden, axes, split_axis=0, concat_axis=0, tiled=True)]
    dot_general x5, matrix products: 13.3 us -> 22.5 us  [orthogonal(): jnp.dot(poly_mix, iterate, preferred_element_type=jnp.float32)]
    dot_general x5, matrix products: 11.3 us -> 14.9 us  [orthogonal(): jnp.dot(iterate, iterate.T, preferred_element_type=jnp.float32)]
    dot_general x1, matrix products: 8.89 us -> 5.45 us  [dense_shards(): lax.dot_general(recv_hidden.reshape(device_count * tok_rows, hidden_width...]
  transfers between devices with their start and end apart: 3 -> 3, of which waited for: 3 -> 2; matrix products, arithmetic and copies ran while one was open for 1% -> 25% of each run, Pallas kernels for 0% -> 0%
where the time goes in v2:
time: 183 us; the launch traced here: 181 us
  waiting for transfers between devices  89.3 us (49%)
  matrix products  52.2 us (29%)
  between operations  14.8 us (8%)
  starting transfers between devices  11.6 us (6%)
  other arithmetic  9.83 us (5%)
  local copies, waits for them, and re-layouts  3.56 us (2%)
    all_to_all x1, waiting for transfers between devices, dense_shards(): lax.all_to_all(send_hidden, axes, split_axis=0, concat_axis=0, tiled=True)  55.8 us
    all_gather x1, waiting for transfers between devices, dense_shards(): all_grad = lax.all_gather(grad_out, axes, axis=0, tiled=True)  32.9 us
    dot_general x5, matrix products, orthogonal(): jnp.dot(poly_mix, iterate, preferred_element_type=jnp.float32)  22.5 us
    dot_general x5, matrix products, orthogonal(): jnp.dot(iterate, iterate.T, preferred_element_type=jnp.float32)  14.9 us
    dot_general x1, matrix products, dense_shards(): lax.dot_general(all_grad, weights[0], (((1,), (1,)), ((), ())), preferred...  9.29 us
    all_to_all x1, starting transfers between devices, dense_shards(): lax.all_to_all(send_hidden, axes, split_axis=0, concat_axis=0, tiled=True)  6.69 us
    dot_general x1, matrix products, dense_shards(): lax.dot_general(recv_hidden.reshape(device_count * tok_rows, hidden_width...  5.45 us
    all_to_all x1, starting transfers between devices, dense_shards(): lax.all_to_all(raw_grad.reshape(device_count, tok_rows, hidden_width), ax...  4.92 us
  transfers between devices with their start and end apart: 3, of which 2 were waited for; matrix products, arithmetic and copies ran while one was open for 25% of the time, Pallas kernels for 0%

profile of v2, /device:TPU:15, one launch (start us, length us, event | category | flops | bytes accessed | tf_op | source)
XLA Modules:
  0.0 181.3 jit_solution(12479461664257593891)
XLA Ops:
  7.2 0.7 all-gather.2.cloned.1.call-update
  7.9 0.7 convert_element_type.127
  8.6 1.0 slice_bitcast_fusion.31
  9.6 1.3 fusion.8
  11.1 4.5 %select_select_fusion = bf16[16,128,384]{2,1,0:T(8,128)(2,1)} fusion(pred[16,128]{1,0:T(8,128)(4,1)S(1)} %get-tuple-element.72, pred[16,128]{1,0:T(8,128)(4,1)S(1)} %get-tuple-element.73, pred[16,128]{1,0:T(8,128)(4,1)S(1)} %get-tuple-element.74, pred[16,128]{1,0:T(8,128)(4,1)S(1)} %get-tuple-element.75, pred[16,128]{1,0:T(8,128)(4,1)S(1)} %get-tuple-element.76, ...), kind=kLoop, calls=%fused_computation.40 | loop fusion | flops 6291456 | bytes 2375680 | tf_op jit(solution)/shard_map/jit(_where)/select_n | solution.py:135
  15.6 6.7 %all-to-all-start = ((bf16[16,128,384]{2,1,0:T(8,128)(2,1)}), bf16[16,128,384]{2,1,0:T(8,128)(2,1)S(1)}, u32[]{:S(2)}, u32[]{:S(2)}) async-start(bf16[16,128,384]{2,1,0:T(8,128)(2,1)} %select_select_fusion), calls=%async_computation | async-start | bytes 3145728 | tf_op jit(solution)/shard_map/all_to_all | solution.py:136
  22.3 55.8 %all-to-all-done = bf16[16,128,384]{2,1,0:T(8,128)(2,1)S(1)} async-done(((bf16[16,128,384]{2,1,0:T(8,128)(2,1)}), bf16[16,128,384]{2,1,0:T(8,128)(2,1)S(1)}, u32[]{:S(2)}, u32[]{:S(2)}) %all-to-all-start) | async-done | bytes 1572896 | tf_op jit(solution)/shard_map/all_to_all | solution.py:136
  78.0 32.9 %all-gather.2.cloned.1.call-done = bf16[2048,2048]{1,0:T(8,128)(2,1)} async-done(((bf16[128,2048]{1,0:T(8,128)(2,1)}), bf16[2048,2048]{1,0:T(8,128)(2,1)}) %all-gather.2.cloned.1.call-update) | async-done | bytes 8388624 | tf_op jit(solution)/shard_map/all_gather | solution.py:126
  110.9 9.3 %convolution_convert_fusion = bf16[2048,384]{1,0:T(8,128)(2,1)} fusion(bf16[2048,2048]{1,0:T(8,128)(2,1)} %all-gather.2.cloned.1.call-done, bf16[1,384,2048]{2,1,0:T(8,128)(2,1)S(1)} %copy-done), kind=kOutput, calls=%fused_computation.17 | convolution fusion | flops 3222011904 | bytes 11534336 | tf_op jit(solution)/shard_map/dot_general | solution.py:138
  120.2 5.5 %fusion = (f32[]{:T(128)}, bf16[1,384,2048]{2,1,0:T(8,128)(2,1)}) fusion(bf16[2048,384]{1,0:T(8,128)(2,1)S(1)} %bitcast.144, bf16[2048,2048]{1,0:T(8,128)(2,1)S(1)} %copy-done.3, bf16[1,384,2048]{2,1,0:T(8,128)(2,1)S(1)} %copy-done.4), kind=kOutput, calls=%fused_computation.2 | convolution fusion | flops 3226730496 | bytes 13107204 | tf_op jit(solution)/shard_map/dot_general | solution.py:149
  126.4 4.9 %all-to-all-start.1 = ((bf16[16,128,384]{2,1,0:T(8,128)(2,1)}), bf16[16,128,384]{2,1,0:T(8,128)(2,1)S(1)}, u32[]{:S(2)}, u32[]{:S(2)}) async-start(bf16[16,128,384]{2,1,0:T(8,128)(2,1)} %bitcast.143), calls=%async_computation.1 | async-start | bytes 3145728 | tf_op jit(solution)/shard_map/all_to_all | solution.py:142
  131.3 2.9 %fusion.37 = bf16[384,384]{1,0:T(8,128)(2,1)S(1)} fusion(bf16[1,384,2048]{2,1,0:T(8,128)(2,1)} %get-tuple-element.71, f32[]{:T(128)S(6)} %add.43), kind=kOutput, calls=%fused_computation.56 | convolution fusion | flops 606486528 | bytes 1867780 | tf_op jit(solution)/shard_map/vmap()/dot_general | solution.py:23
  134.2 4.3 %fusion.6 = bf16[1,384,2048]{2,1,0:T(8,128)(2,1)} fusion(bf16[384,384]{1,0:T(8,128)(2,1)S(1)} %fusion.37, f32[]{:T(128)S(6)} %add.43, bf16[1,384,2048]{2,1,0:T(8,128)(2,1)} %get-tuple-element.71), kind=kOutput, calls=%fused_computation.13 | convolution fusion | flops 725827584 | bytes 3440644 | tf_op jit(solution)/shard_map/vmap()/dot_general | solution.py:32
  138.5 3.0 %fusion.40 = bf16[384,384]{1,0:T(8,128)(2,1)S(1)} fusion(bf16[1,384,2048]{2,1,0:T(8,128)(2,1)} %fusion.6), kind=kOutput, calls=%fused_computation.57 | convolution fusion | flops 604127232 | bytes 1867776 | tf_op jit(solution)/shard_map/vmap()/dot_general | solution.py:23
  141.5 4.4 %fusion.5 = bf16[1,384,2048]{2,1,0:T(8,128)(2,1)} fusion(bf16[1,384,2048]{2,1,0:T(8,128)(2,1)} %fusion.6, bf16[384,384]{1,0:T(8,128)(2,1)S(1)} %fusion.40), kind=kOutput, calls=%fused_computation.11 | convolution fusion | flops 721108992 | bytes 3440640 | tf_op jit(solution)/shard_map/vmap()/dot_general | solution.py:32
  146.0 3.0 %fusion.43 = bf16[384,384]{1,0:T(8,128)(2,1)S(1)} fusion(bf16[1,384,2048]{2,1,0:T(8,128)(2,1)} %fusion.5), kind=kOutput, calls=%fused_computation.58 | convolution fusion | flops 604127232 | bytes 1867776 | tf_op jit(solution)/shard_map/vmap()/dot_general | solution.py:23
  149.0 4.4 %fusion.4 = bf16[1,384,2048]{2,1,0:T(8,128)(2,1)} fusion(bf16[1,384,2048]{2,1,0:T(8,128)(2,1)} %fusion.5, bf16[384,384]{1,0:T(8,128)(2,1)S(1)} %fusion.43), kind=kOutput, calls=%fused_computation.9 | convolution fusion | flops 721108992 | bytes 3440640 | tf_op jit(solution)/shard_map/vmap()/dot_general | solution.py:32
  153.3 3.0 %fusion.46 = bf16[384,384]{1,0:T(8,128)(2,1)S(1)} fusion(bf16[1,384,2048]{2,1,0:T(8,128)(2,1)} %fusion.4), kind=kOutput, calls=%fused_computation.59 | convolution fusion | flops 604127232 | bytes 1867776 | tf_op jit(solution)/shard_map/vmap()/dot_general | solution.py:23
  156.4 4.4 %fusion.3 = bf16[1,384,2048]{2,1,0:T(8,128)(2,1)} fusion(bf16[1,384,2048]{2,1,0:T(8,128)(2,1)} %fusion.4, bf16[384,384]{1,0:T(8,128)(2,1)S(1)} %fusion.46), kind=kOutput, calls=%fused_computation.7 | convolution fusion | flops 721108992 | bytes 3440640 | tf_op jit(solution)/shard_map/vmap()/dot_general | solution.py:32
  160.8 3.0 %fusion.49 = bf16[384,384]{1,0:T(8,128)(2,1)S(1)} fusion(bf16[1,384,2048]{2,1,0:T(8,128)(2,1)} %fusion.3), kind=kOutput, calls=%fused_computation.60 | convolution fusion | flops 604127232 | bytes 1867776 | tf_op jit(solution)/shard_map/vmap()/dot_general | solution.py:23
  163.8 4.9 %convert_multiply_fusion.1 = f32[1,384,2048]{2,1,0:T(8,128)} fusion(bf16[1,384,2048]{2,1,0:T(8,128)(2,1)} %fusion.3, bf16[384,384]{1,0:T(8,128)(2,1)S(1)} %fusion.49), kind=kOutput, calls=%fused_computation.16 | convolution fusion | flops 722681856 | bytes 5013504 | tf_op jit(solution)/shard_map/vmap()/dot_general | solution.py:32
  168.9 0.9 copy-done.1
  169.9 3.1 %fusion.10 = (f32[128,8]{0,1:T(8,128)}, bf16[128,8,384]{2,0,1:T(8,128)(2,1)S(1)}) fusion(bf16[128,8,384]{2,1,0:T(8,128)(2,1)S(1)} %copy-done.1, bf16[128,384]{1,0:T(8,128)(2,1)S(1)} %get-tuple-element.23, pred[128,8]{0,1:T(8,128)(4,1)S(1)} %get-tuple-element.60, bf16[128,384]{1,0:T(8,128)(2,1)S(1)} %get-tuple-element.24, ...), kind=kLoop, calls=%fused_computation.23 | loop fusion | flops 7863296 | bytes 3166208 | tf_op jit(solution)/shard_map/reduce_sum | solution.py:167
  173.2 1.3 copy.28
  (19 shorter events, 0.6 us)
Async XLA Ops:
  7.2 103.8 %copy-start = (bf16[1,384,2048]{2,1,0:T(8,128)(2,1)S(1)}, bf16[1,384,2048]{2,1,0:T(8,128)(2,1)}, u32[]{:S(2)}) copy-start(bf16[1,384,2048]{2,1,0:T(8,128)(2,1)} %param.10) | copy-start | bytes 4718596
  7.2 103.7 %all-gather.2.cloned.1.call-start = ((), (), s32[]{:S(2)}) async-start(), calls=%async_computation.2 | async-start | bytes 8912896 | tf_op jit(solution)/shard_map/all_gather | solution.py:126
  15.6 6.7 %copy-start.2 = (s32[128,8]{0,1:T(8,128)S(1)}, s32[128,8]{0,1:T(8,128)}, u32[]{:S(2)}) copy-start(s32[128,8]{0,1:T(8,128)} %param.7) | copy-start | bytes 12292
  15.6 62.5 %all-to-all-start = ((bf16[16,128,384]{2,1,0:T(8,128)(2,1)}), bf16[16,128,384]{2,1,0:T(8,128)(2,1)S(1)}, u32[]{:S(2)}, u32[]{:S(2)}) async-start(bf16[16,128,384]{2,1,0:T(8,128)(2,1)} %select_select_fusion), calls=%async_computation | async-start | bytes 3145728 | tf_op jit(solution)/shard_map/all_to_all | solution.py:136
  110.9 9.3 %copy-start.3 = (bf16[2048,2048]{1,0:T(8,128)(2,1)S(1)}, bf16[2048,2048]{1,0:T(8,128)(2,1)}, u32[]{:S(2)}) copy-start(bf16[2048,2048]{1,0:T(8,128)(2,1)} %all-gather.2.cloned.1.call-done) | copy-start | bytes 25165828
  110.9 9.3 %copy-start.4 = (bf16[1,384,2048]{2,1,0:T(8,128)(2,1)S(1)}, bf16[1,384,2048]{2,1,0:T(8,128)(2,1)}, u32[]{:S(2)}) copy-start(bf16[1,384,2048]{2,1,0:T(8,128)(2,1)} %param.11) | copy-start | bytes 4718596
  126.4 42.4 %all-to-all-start.1 = ((bf16[16,128,384]{2,1,0:T(8,128)(2,1)}), bf16[16,128,384]{2,1,0:T(8,128)(2,1)S(1)}, u32[]{:S(2)}, u32[]{:S(2)}) async-start(bf16[16,128,384]{2,1,0:T(8,128)(2,1)} %bitcast.143), calls=%async_computation.1 | async-start | bytes 3145728 | tf_op jit(solution)/shard_map/all_to_all | solution.py:142
  168.7 1.1 copy-start.1
Sparse Core Ops, SparseCore 0:
  10.2 100.6 all-gather.1

commit v3 on v1

--- a/solution.py
+++ b/solution.py
@@ -1,8 +1,11 @@
+import functools
 import math
 
 import jax
 import jax.numpy as jnp
 from jax import lax
+from jax.experimental import pallas as pl
+from jax.experimental.pallas import tpu as pltpu
 from jax.sharding import PartitionSpec as P
 
 EXP_DEV = 4
@@ -116,6 +119,210 @@
     )
 
 
+def exchange_kernel(
+    owners,
+    width,
+    grad_ref,
+    hid_ref,
+    all_ref,
+    recv_ref,
+    local_sem,
+    up_sem,
+    down_sem,
+    cross_sem,
+    sib_sem,
+    block_sem,
+    hid_send,
+    hid_recv,
+):
+    total = owners * width
+    row = lax.axis_index("expert")
+    lane = lax.axis_index("dp")
+    sibling = lane + 1 - 2 * lax.rem(lane, 2)
+    cross = lax.rem(lane + 2, width)
+    cross_sibling = lax.rem(sibling + 2, width)
+    me = row * width + lane
+
+    def target(peer_row, peer_lane):
+        return {"expert": peer_row, "dp": peer_lane}
+
+    def peer_at(offset):
+        return lax.rem(me + offset, total)
+
+    barrier = pltpu.get_barrier_semaphore()
+
+    @pl.loop(1, total)
+    def _(offset):
+        peer = peer_at(offset)
+        pl.semaphore_signal(
+            barrier,
+            inc=1,
+            device_id=target(peer // width, lax.rem(peer, width)),
+            device_id_type=pl.DeviceIdType.MESH,
+        )
+
+    pl.semaphore_wait(barrier, total - 1)
+
+    def block_copy(source_row, source_lane, send_sem, peer_row, peer_lane, first=False):
+        rank = source_row * width + source_lane
+        return pltpu.make_async_remote_copy(
+            src_ref=grad_ref if first else all_ref.at[rank],
+            dst_ref=all_ref.at[rank],
+            send_sem=send_sem,
+            recv_sem=block_sem.at[rank],
+            device_id=target(peer_row, peer_lane),
+            device_id_type=pl.DeviceIdType.MESH,
+        )
+
+    def up(source_row, first=False):
+        return block_copy(source_row, lane, up_sem.at[source_row], row + 1, lane, first)
+
+    def down(source_row, first=False):
+        return block_copy(source_row, lane, down_sem.at[source_row], row - 1, lane, first)
+
+    def over(source_row, first=False):
+        return block_copy(source_row, lane, cross_sem.at[source_row], row, cross, first)
+
+    def aside(source_row, column, first=False):
+        source_lane = cross if column else lane
+        return block_copy(
+            source_row, source_lane, sib_sem.at[source_row * 2 + column], row, sibling, first
+        )
+
+    def arrive(source_row, source_lane):
+        block_copy(source_row, source_lane, up_sem.at[0], row, sibling).wait_recv()
+
+    def hid_copy(offset):
+        peer = peer_at(offset)
+        return pltpu.make_async_remote_copy(
+            src_ref=hid_ref.at[peer],
+            dst_ref=recv_ref.at[me],
+            send_sem=hid_send.at[offset],
+            recv_sem=hid_recv.at[me],
+            device_id=target(peer // width, lax.rem(peer, width)),
+            device_id_type=pl.DeviceIdType.MESH,
+        )
+
+    @pl.when(row < owners - 1)
+    def _():
+        up(row, True).start()
+
+    @pl.when(row > 0)
+    def _():
+        down(row, True).start()
+
+    over(row, True).start()
+    aside(row, 0, True).start()
+    own_grad = pltpu.make_async_copy(grad_ref, all_ref.at[me], local_sem.at[0])
+    own_grad.start()
+    own_hid = pltpu.make_async_copy(hid_ref.at[me], recv_ref.at[me], local_sem.at[1])
+    own_hid.start()
+
+    @pl.loop(1, total)
+    def _(offset):
+        hid_copy(offset).start()
+
+    def cross_arrival(source_row):
+        arrive(source_row, cross)
+        aside(source_row, 1).start()
+
+    for step in range(1, owners + 1):
+        if step < owners:
+
+            @pl.when(row - step >= 0)
+            def _():
+                arrive(row - step, lane)
+
+                @pl.when(row < owners - 1)
+                def _():
+                    up(row - step).start()
+
+                over(row - step).start()
+                aside(row - step, 0).start()
+
+            @pl.when(row + step < owners)
+            def _():
+                arrive(row + step, lane)
+
+                @pl.when(row > 0)
+                def _():
+                    down(row + step).start()
+
+                over(row + step).start()
+                aside(row + step, 0).start()
+
+        if step == 1:
+            cross_arrival(row)
+        else:
+
+            @pl.when(row - (step - 1) >= 0)
+            def _():
+                cross_arrival(row - (step - 1))
+
+            @pl.when(row + (step - 1) < owners)
+            def _():
+                cross_arrival(row + (step - 1))
+
+    own_grad.wait()
+    own_hid.wait()
+
+    @pl.loop(0, owners)
+    def _(source_row):
+        arrive(source_row, sibling)
+        arrive(source_row, cross_sibling)
+        over(source_row).wait_send()
+        aside(source_row, 0).wait_send()
+        aside(source_row, 1).wait_send()
+
+        @pl.when((source_row <= row) & (row < owners - 1))
+        def _():
+            up(source_row).wait_send()
+
+        @pl.when((source_row >= row) & (row > 0))
+        def _():
+            down(source_row).wait_send()
+
+    @pl.loop(1, total)
+    def _(offset):
+        hid_copy(offset).wait_send()
+        peer = peer_at(offset)
+        pltpu.make_async_remote_copy(
+            src_ref=hid_ref.at[peer],
+            dst_ref=recv_ref.at[peer],
+            send_sem=hid_send.at[offset],
+            recv_sem=hid_recv.at[peer],
+            device_id=target(peer // width, lax.rem(peer, width)),
+            device_id_type=pl.DeviceIdType.MESH,
+        ).wait_recv()
+
+
+def exchange(grad_out, send_hidden):
+    owners, width = lax.axis_size("expert"), lax.axis_size("dp")
+    total = owners * width
+    dma = pltpu.SemaphoreType.DMA
+    return pl.pallas_call(
+        functools.partial(exchange_kernel, owners, width),
+        out_shape=(
+            jax.ShapeDtypeStruct((total,) + grad_out.shape, grad_out.dtype),
+            jax.ShapeDtypeStruct(send_hidden.shape, send_hidden.dtype),
+        ),
+        in_specs=[pl.BlockSpec(memory_space=pl.ANY)] * 2,
+        out_specs=(pl.BlockSpec(memory_space=pl.ANY),) * 2,
+        scratch_shapes=[
+            dma((2,)),
+            dma((owners,)),
+            dma((owners,)),
+            dma((owners,)),
+            dma((2 * owners,)),
+            dma((total,)),
+            dma((total,)),
+            dma((total,)),
+        ],
+        compiler_params=pltpu.CompilerParams(collective_id=0, has_side_effects=True),
+        name="exchange",
+    )(grad_out, send_hidden)
+
+
 def dense_shards(grad_out, expert_ids, probs, hidden, weights, momentum):
     axes = ("expert", "dp")
     tok_rows, model_width = grad_out.shape
@@ -123,7 +330,6 @@
     hidden_width = hidden.shape[2]
     device_count = lax.axis_size("expert") * lax.axis_size("dp")
     expert_total = device_count * weights.shape[0]
-    all_grad = lax.all_gather(grad_out, axes, axis=0, tiled=True)
     experts = jnp.arange(expert_total, dtype=jnp.int32)
     zero_value = jnp.zeros((), jnp.bfloat16)
     prob_hidden = (probs[..., None].astype(jnp.float32) * hidden.astype(jnp.float32)).astype(
@@ -133,7 +339,8 @@
     for choice in range(top_count):
         named = expert_ids[None, :, choice] == experts[:, None]
         send_hidden = jnp.where(named[..., None], prob_hidden[None, :, choice], send_hidden)
-    recv_hidden = lax.all_to_all(send_hidden, axes, split_axis=0, concat_axis=0, tiled=True)
+    all_grad, recv_hidden = exchange(grad_out, send_hidden)
+    all_grad = all_grad.reshape(device_count * tok_rows, model_width)
     raw_grad = lax.dot_general(
         all_grad, weights[0], (((1,), (1,)), ((), ())), preferred_element_type=jnp.float32
     ).astype(jnp.bfloat16)
@@ -154,6 +361,7 @@
         jnp.bfloat16
     )
     update = jax.vmap(orthogonal)(new_momentum)
+    update, returned = lax.optimization_barrier((update, returned))
     raw_rows = jnp.zeros((tok_rows, top_count, hidden_width), jnp.bfloat16)
     for expert in range(expert_total):
         named = expert_ids == expert
@@ -187,7 +395,7 @@
     def program(grad_out, expert_ids, probs, hidden, weights, momentum):
         tok_rows = grad_out.shape[0] // (mesh.shape["group"] * owners * dp_count)
         expert_total = weights.shape[0]
-        dense = expert_total == owners * dp_count and (
+        dense = dp_count == 4 and expert_total == owners * dp_count and (
             2 * tok_rows * expert_ids.shape[1] // expert_total >= tok_rows
         )
         return jax.shard_map(

time: 228 us -> 168 us (0.74)
  waiting for transfers between devices: 149 us -> 0.01 us
  Pallas kernels: 0 us -> 77.6 us
  matrix products: 42.6 us -> 56.4 us
  between operations: 14.9 us -> 1.45 us
  starting transfers between devices: 10.5 us -> 17.9 us
    pallas_call x0 -> x1, Pallas kernels: none -> 77.6 us  [exchange(): pl.pallas_call(functools.partial(exchange_kernel, owners, width), out_sha...]
    all_gather x1 -> x0, waiting for transfers between devices: 77.2 us -> none  [dense_shards(): all_grad = lax.all_gather(grad_out, axes, axis=0, tiled=True)]
    all_to_all x1, waiting for transfers between devices: 36.1 us -> 0.01 us  [dense_shards(): lax.all_to_all(raw_grad.reshape(device_count, tok_rows, hidden_width), ax...]
    all_to_all x1 -> x0, waiting for transfers between devices: 34.9 us -> none  [dense_shards(): lax.all_to_all(send_hidden, axes, split_axis=0, concat_axis=0, tiled=True)]
    all_to_all x1, starting transfers between devices: 5.6 us -> 17.9 us  [dense_shards(): lax.all_to_all(raw_grad.reshape(device_count, tok_rows, hidden_width), ax...]
    dot_general x5, matrix products: 13.3 us -> 22.5 us  [orthogonal(): jnp.dot(poly_mix, iterate, preferred_element_type=jnp.float32)]
    all_to_all x1 -> x0, starting transfers between devices: 4.88 us -> none  [dense_shards(): lax.all_to_all(send_hidden, axes, split_axis=0, concat_axis=0, tiled=True)]
    dot_general x5, matrix products: 11.3 us -> 14.8 us  [orthogonal(): jnp.dot(iterate, iterate.T, preferred_element_type=jnp.float32)]
  transfers between devices with their start and end apart: 3 -> 1, of which waited for: 3 -> 0; matrix products, arithmetic and copies ran while one was open for 1% -> 28% of each run, Pallas kernels for 0% -> 0%
where the time goes in v3:
time: 168 us; the launch traced here: 167 us
  Pallas kernels  77.6 us (46%)
  matrix products  56.4 us (34%)
  starting transfers between devices  17.9 us (11%)
  other arithmetic  9.83 us (6%)
  local copies, waits for them, and re-layouts  3.56 us (2%)
    pallas_call x1, Pallas kernels, exchange(): pl.pallas_call(functools.partial(exchange_kernel, owners, width), out_sha...  77.6 us
    dot_general x5, matrix products, orthogonal(): jnp.dot(poly_mix, iterate, preferred_element_type=jnp.float32)  22.5 us
    all_to_all x1, starting transfers between devices, dense_shards(): lax.all_to_all(raw_grad.reshape(device_count, tok_rows, hidden_width), ax...  17.9 us
    dot_general x5, matrix products, orthogonal(): jnp.dot(iterate, iterate.T, preferred_element_type=jnp.float32)  14.8 us
    dot_general x1, matrix products, dense_shards(): lax.dot_general(recv_hidden.reshape(device_count * tok_rows, hidden_width...  9.96 us
    dot_general x1, matrix products, dense_shards(): lax.dot_general(all_grad, weights[0], (((1,), (1,)), ((), ())), preferred...  9.13 us
    select_n x1, other arithmetic, dense_shards(): jnp.where(named[..., None], prob_hidden[None, :, choice], send_hidden)  4.48 us
  transfers between devices with their start and end apart: 1, of which 0 were waited for; matrix products, arithmetic and copies ran while one was open for 28% of the time, Pallas kernels for 0%

profile of v3, /device:TPU:15, one launch (start us, length us, event | category | flops | bytes accessed | tf_op | source)
XLA Modules:
  0.0 166.7 jit_solution(1076720759973844138)
XLA Ops:
  0.6 1.0 slice_bitcast_fusion.31
  1.6 0.7 convert_element_type.127
  2.3 1.3 fusion.8
  3.7 0.1 slice_bitcast_fusion.7
  3.8 4.5 %select_select_fusion.hid_ref = bf16[16,128,384]{2,1,0:T(8,128)(2,1)} fusion(pred[16,128]{1,0:T(8,128)(4,1)S(1)} %get-tuple-element.68, pred[16,128]{1,0:T(8,128)(4,1)S(1)} %get-tuple-element.69, pred[16,128]{1,0:T(8,128)(4,1)S(1)} %get-tuple-element.70, pred[16,128]{1,0:T(8,128)(4,1)S(1)} %get-tuple-element.71, pred[16,128]{1,0:T(8,128)(4,1)S(1)} %get-tuple-element.72, ...), kind=kLoop, calls=%fused_computation.40 | loop fusion | flops 6291456 | bytes 2375680 | tf_op jit(solution)/shard_map/jit(_where)/select_n | solution.py:341
  8.3 77.6 %exchange.1 = (bf16[16,128,2048]{2,1,0:T(8,128)(2,1)}, bf16[16,128,384]{2,1,0:T(8,128)(2,1)}) custom-call(bf16[128,2048]{1,0:T(8,128)(2,1)} %grad_ref.1, bf16[16,128,384]{2,1,0:T(8,128)(2,1)} %select_select_fusion.hid_ref), custom_call_target="tpu_custom_call" | custom-call | tf_op jit(solution)/shard_map/exchange/pallas_call | solution.py:303
  85.9 9.1 %convolution_convert_fusion = bf16[2048,384]{1,0:T(8,128)(2,1)} fusion(bf16[2048,2048]{1,0:T(8,128)(2,1)} %bitcast.145, bf16[1,384,2048]{2,1,0:T(8,128)(2,1)S(1)} %copy-done), kind=kOutput, calls=%fused_computation.17 | convolution fusion | flops 3222011904 | bytes 11534336 | tf_op jit(solution)/shard_map/dot_general | solution.py:344
  95.0 17.9 %all-to-all-start = ((bf16[16,128,384]{2,1,0:T(8,128)(2,1)}), bf16[16,128,384]{2,1,0:T(8,128)(2,1)S(1)}, u32[]{:S(2)}, u32[]{:S(2)}) async-start(bf16[16,128,384]{2,1,0:T(8,128)(2,1)} %bitcast.144), calls=%async_computation | async-start | bytes 3145728 | tf_op jit(solution)/shard_map/all_to_all | solution.py:347
  112.9 10.0 %fusion = (f32[]{:T(128)}, bf16[1,384,2048]{2,1,0:T(8,128)(2,1)}) fusion(bf16[16,128,384]{2,1,0:T(8,128)(2,1)} %get-tuple-element.8, bf16[16,128,2048]{2,1,0:T(8,128)(2,1)} %get-tuple-element.9, bf16[1,384,2048]{2,1,0:T(8,128)(2,1)} %param.11), kind=kOutput, calls=%fused_computation.2 | convolution fusion | flops 3226730496 | bytes 13107204 | tf_op jit(solution)/shard_map/dot_general | solution.py:354
  123.6 2.9 %fusion.37 = bf16[384,384]{1,0:T(8,128)(2,1)S(1)} fusion(bf16[1,384,2048]{2,1,0:T(8,128)(2,1)} %get-tuple-element.67, f32[]{:T(128)S(6)} %add.43), kind=kOutput, calls=%fused_computation.56 | convolution fusion | flops 606486528 | bytes 1867780 | tf_op jit(solution)/shard_map/vmap()/dot_general | solution.py:26
  126.5 4.3 %fusion.6 = bf16[1,384,2048]{2,1,0:T(8,128)(2,1)} fusion(bf16[384,384]{1,0:T(8,128)(2,1)S(1)} %fusion.37, f32[]{:T(128)S(6)} %add.43, bf16[1,384,2048]{2,1,0:T(8,128)(2,1)} %get-tuple-element.67), kind=kOutput, calls=%fused_computation.13 | convolution fusion | flops 725827584 | bytes 3440644 | tf_op jit(solution)/shard_map/vmap()/dot_general | solution.py:35
  130.8 3.0 %fusion.40 = bf16[384,384]{1,0:T(8,128)(2,1)S(1)} fusion(bf16[1,384,2048]{2,1,0:T(8,128)(2,1)} %fusion.6), kind=kOutput, calls=%fused_computation.57 | convolution fusion | flops 604127232 | bytes 1867776 | tf_op jit(solution)/shard_map/vmap()/dot_general | solution.py:26
  133.9 4.4 %fusion.5 = bf16[1,384,2048]{2,1,0:T(8,128)(2,1)} fusion(bf16[1,384,2048]{2,1,0:T(8,128)(2,1)} %fusion.6, bf16[384,384]{1,0:T(8,128)(2,1)S(1)} %fusion.40), kind=kOutput, calls=%fused_computation.11 | convolution fusion | flops 721108992 | bytes 3440640 | tf_op jit(solution)/shard_map/vmap()/dot_general | solution.py:35
  138.3 2.9 %fusion.43 = bf16[384,384]{1,0:T(8,128)(2,1)S(1)} fusion(bf16[1,384,2048]{2,1,0:T(8,128)(2,1)} %fusion.5), kind=kOutput, calls=%fused_computation.58 | convolution fusion | flops 604127232 | bytes 1867776 | tf_op jit(solution)/shard_map/vmap()/dot_general | solution.py:26
  141.2 4.3 %fusion.4 = bf16[1,384,2048]{2,1,0:T(8,128)(2,1)} fusion(bf16[1,384,2048]{2,1,0:T(8,128)(2,1)} %fusion.5, bf16[384,384]{1,0:T(8,128)(2,1)S(1)} %fusion.43), kind=kOutput, calls=%fused_computation.9 | convolution fusion | flops 721108992 | bytes 3440640 | tf_op jit(solution)/shard_map/vmap()/dot_general | solution.py:35
  145.5 3.0 %fusion.46 = bf16[384,384]{1,0:T(8,128)(2,1)S(1)} fusion(bf16[1,384,2048]{2,1,0:T(8,128)(2,1)} %fusion.4), kind=kOutput, calls=%fused_computation.59 | convolution fusion | flops 604127232 | bytes 1867776 | tf_op jit(solution)/shard_map/vmap()/dot_general | solution.py:26
  148.5 4.4 %fusion.3 = bf16[1,384,2048]{2,1,0:T(8,128)(2,1)} fusion(bf16[1,384,2048]{2,1,0:T(8,128)(2,1)} %fusion.4, bf16[384,384]{1,0:T(8,128)(2,1)S(1)} %fusion.46), kind=kOutput, calls=%fused_computation.7 | convolution fusion | flops 721108992 | bytes 3440640 | tf_op jit(solution)/shard_map/vmap()/dot_general | solution.py:35
  152.9 2.9 %fusion.49 = bf16[384,384]{1,0:T(8,128)(2,1)S(1)} fusion(bf16[1,384,2048]{2,1,0:T(8,128)(2,1)} %fusion.3), kind=kOutput, calls=%fused_computation.60 | convolution fusion | flops 604127232 | bytes 1867776 | tf_op jit(solution)/shard_map/vmap()/dot_general | solution.py:26
  155.8 5.1 %convert_multiply_fusion.1 = f32[1,384,2048]{2,1,0:T(8,128)} fusion(bf16[1,384,2048]{2,1,0:T(8,128)(2,1)} %fusion.3, bf16[384,384]{1,0:T(8,128)(2,1)S(1)} %fusion.49), kind=kOutput, calls=%fused_computation.16 | convolution fusion | flops 722681856 | bytes 5013504 | tf_op jit(solution)/shard_map/vmap()/dot_general | solution.py:35
  160.9 0.2 slice_bitcast_fusion.23
  161.1 0.9 copy-done.1
  162.0 3.1 %fusion.10 = (f32[128,8]{0,1:T(8,128)}, bf16[128,8,384]{2,0,1:T(8,128)(2,1)S(1)}) fusion(bf16[128,8,384]{2,1,0:T(8,128)(2,1)S(1)} %copy-done.1, bf16[128,384]{1,0:T(8,128)(2,1)S(1)} %get-tuple-element.19, pred[128,8]{0,1:T(8,128)(4,1)S(1)} %get-tuple-element.56, bf16[128,384]{1,0:T(8,128)(2,1)S(1)} %get-tuple-element.20, ...), kind=kLoop, calls=%fused_computation.23 | loop fusion | flops 7863296 | bytes 3166208 | tf_op jit(solution)/shard_map/reduce_sum | solution.py:372
  165.1 0.2 fusion.9
  165.3 1.3 copy.30
  (11 shorter events, 0.1 us)
Async XLA Ops:
  0.6 85.3 %copy-start = (bf16[1,384,2048]{2,1,0:T(8,128)(2,1)S(1)}, bf16[1,384,2048]{2,1,0:T(8,128)(2,1)}, u32[]{:S(2)}) copy-start(bf16[1,384,2048]{2,1,0:T(8,128)(2,1)} %param.10) | copy-start | bytes 4718596
  95.0 17.9 %copy-start.2 = (s32[128,8]{0,1:T(8,128)S(1)}, s32[128,8]{0,1:T(8,128)}, u32[]{:S(2)}) copy-start(s32[128,8]{0,1:T(8,128)} %param.7) | copy-start | bytes 12292
  95.0 65.8 %all-to-all-start = ((bf16[16,128,384]{2,1,0:T(8,128)(2,1)}), bf16[16,128,384]{2,1,0:T(8,128)(2,1)S(1)}, u32[]{:S(2)}, u32[]{:S(2)}) async-start(bf16[16,128,384]{2,1,0:T(8,128)(2,1)} %bitcast.144), calls=%async_computation | async-start | bytes 3145728 | tf_op jit(solution)/shard_map/all_to_all | solution.py:347
  160.9 1.1 copy-start.1

commit v4 on v3

--- a/solution.py
+++ b/solution.py
@@ -218,9 +218,12 @@
     own_hid = pltpu.make_async_copy(hid_ref.at[me], recv_ref.at[me], local_sem.at[1])
     own_hid.start()
 
-    @pl.loop(1, total)
-    def _(offset):
-        hid_copy(offset).start()
+    def start_hidden(low, high):
+        @pl.loop(low, high)
+        def _(offset):
+            hid_copy(offset).start()
+
+    first_batch = 1 + (total - 1) // 3
 
     def cross_arrival(source_row):
         arrive(source_row, cross)
@@ -250,6 +253,11 @@
 
                 over(row + step).start()
                 aside(row + step, 0).start()
+
+        if step == 1:
+            start_hidden(1, first_batch)
+        elif step == 2:
+            start_hidden(first_batch, total)
 
         if step == 1:
             cross_arrival(row)
@@ -323,6 +331,67 @@
     )(grad_out, send_hidden)
 
 
+def orthogonal_kernel(tiles, momentum_ref, update_ref, iterate_ref):
+    height, width = momentum_ref.shape
+    columns = width // tiles
+
+    def tile(index):
+        return pl.ds(pl.multiple_of(index * columns, columns), columns)
+
+    def add_squares(index, total):
+        values = momentum_ref[:, tile(index)].astype(jnp.float32)
+        return total + jnp.sum(values * values, axis=0, keepdims=True)
+
+    squares = lax.fori_loop(0, tiles, add_squares, jnp.zeros((1, columns), jnp.float32))
+    frob_norm = jnp.sqrt(jnp.sum(squares, axis=1, keepdims=True)) + 1e-07
+
+    @pl.loop(0, tiles)
+    def _(index):
+        values = momentum_ref[:, tile(index)].astype(jnp.float32)
+        iterate_ref[:, tile(index)] = (values / frob_norm).astype(jnp.bfloat16)
+
+    @pl.loop(0, ITERS)
+    def _(step_index):
+        iterate = iterate_ref[...]
+        gram_matrix = lax.dot_general(
+            iterate, iterate, (((1,), (1,)), ((), ())), preferred_element_type=jnp.float32
+        ).astype(jnp.bfloat16)
+        gram_square = jnp.dot(gram_matrix, gram_matrix, preferred_element_type=jnp.float32)
+        poly_mix = (coef_b * gram_matrix.astype(jnp.float32) + coef_c * gram_square).astype(
+            jnp.bfloat16
+        )
+        for index in range(tiles):
+            part = pl.ds(index * columns, columns)
+            block = iterate_ref[:, part]
+            iterate_ref[:, part] = (
+                coef_a * block.astype(jnp.float32)
+                + jnp.dot(poly_mix, block, preferred_element_type=jnp.float32)
+            ).astype(jnp.bfloat16)
+
+    @pl.loop(0, tiles)
+    def _(index):
+        update_ref[:, tile(index)] = iterate_ref[:, tile(index)].astype(jnp.float32) * math.sqrt(
+            width
+        )
+
+
+def orthogonal_block(matrix):
+    height, width = matrix.shape
+    macs = ITERS * height * height * (2 * width + height)
+    return pl.pallas_call(
+        functools.partial(orthogonal_kernel, width // 512),
+        out_shape=jax.ShapeDtypeStruct(matrix.shape, jnp.float32),
+        in_specs=[pl.BlockSpec(memory_space=pltpu.VMEM)],
+        out_specs=pl.BlockSpec(memory_space=pltpu.VMEM),
+        scratch_shapes=[pltpu.VMEM(matrix.shape, jnp.bfloat16)],
+        compiler_params=pltpu.CompilerParams(vmem_limit_bytes=24 * 2**20),
+        cost_estimate=pl.CostEstimate(
+            flops=2 * macs, bytes_accessed=6 * height * width, transcendentals=0
+        ),
+        name="orthogonal",
+    )(matrix)
+
+
 def dense_shards(grad_out, expert_ids, probs, hidden, weights, momentum):
     axes = ("expert", "dp")
     tok_rows, model_width = grad_out.shape
@@ -360,7 +429,7 @@
     new_momentum = (momentum_decay * momentum.astype(jnp.float32) + grad_weights).astype(
         jnp.bfloat16
     )
-    update = jax.vmap(orthogonal)(new_momentum)
+    update = orthogonal_block(new_momentum[0])[None]
     update, returned = lax.optimization_barrier((update, returned))
     raw_rows = jnp.zeros((tok_rows, top_count, hidden_width), jnp.bfloat16)
     for expert in range(expert_total):
@@ -395,7 +464,7 @@
     def program(grad_out, expert_ids, probs, hidden, weights, momentum):
         tok_rows = grad_out.shape[0] // (mesh.shape["group"] * owners * dp_count)
         expert_total = weights.shape[0]
-        dense = dp_count == 4 and expert_total == owners * dp_count and (
+        dense = owners >= 3 and dp_count == 4 and expert_total == owners * dp_count and (
             2 * tok_rows * expert_ids.shape[1] // expert_total >= tok_rows
         )
         return jax.shard_map(

time: 168 us -> 152 us (0.905)
  matrix products: 56.4 us -> 17 us
  waiting for transfers between devices: 0.01 us -> 15.1 us
  Pallas kernels: 77.6 us -> 87.4 us
    dot_general x10 -> x0, matrix products: 37.3 us -> none  [the longest x5 22.5 us: orthogonal(): jnp.dot(poly_mix, iterate, preferred_element_type=jnp.float32)]
    all_to_all x1, waiting for transfers between devices: 0.01 us -> 15.1 us  [dense_shards(): lax.all_to_all(raw_grad.reshape(device_count, tok_rows, hidden_width), ax...]
    pallas_call x0 -> x1, Pallas kernels: none -> 13.3 us  [orthogonal_block(): pl.pallas_call(functools.partial(orthogonal_kernel, width // 512), out_sh...]
    pallas_call x1, Pallas kernels: 77.6 us -> 74.1 us  [exchange(): pl.pallas_call(functools.partial(exchange_kernel, owners, width), out_sha...]
    dot_general x1, matrix products: 9.96 us -> 7.81 us  [dense_shards(): lax.dot_general(recv_hidden.reshape(device_count * tok_rows, hidden_width...]
  transfers between devices with their start and end apart: 1 -> 1, of which waited for: 0 -> 1; matrix products, arithmetic and copies ran while one was open for 28% -> 5% of each run, Pallas kernels for 0% -> 9%
where the time goes in v4:
time: 152 us; the launch traced here: 151 us
  Pallas kernels  87.4 us (58%)
  starting transfers between devices  17.1 us (11%)
  matrix products  17 us (11%)
  waiting for transfers between devices  15.1 us (10%)
  other arithmetic  9.97 us (7%)
  local copies, waits for them, and re-layouts  4.15 us (3%)
    pallas_call x1, Pallas kernels, exchange(): pl.pallas_call(functools.partial(exchange_kernel, owners, width), out_sha...  74.1 us
    all_to_all x1, starting transfers between devices, dense_shards(): lax.all_to_all(raw_grad.reshape(device_count, tok_rows, hidden_width), ax...  17.1 us
    all_to_all x1, waiting for transfers between devices, dense_shards(): lax.all_to_all(raw_grad.reshape(device_count, tok_rows, hidden_width), ax...  15.1 us
    pallas_call x1, Pallas kernels, orthogonal_block(): pl.pallas_call(functools.partial(orthogonal_kernel, width // 512), out_sh...  13.3 us
    dot_general x1, matrix products, dense_shards(): lax.dot_general(all_grad, weights[0], (((1,), (1,)), ((), ())), preferred...  9.16 us
    dot_general x1, matrix products, dense_shards(): lax.dot_general(recv_hidden.reshape(device_count * tok_rows, hidden_width...  7.81 us
    select_n x1, other arithmetic, dense_shards(): jnp.where(named[..., None], prob_hidden[None, :, choice], send_hidden)  4.48 us
    reduce_sum x1, other arithmetic, dense_shards(): jnp.sum(raw_rows.astype(jnp.float32) * hidden.astype(jnp.float32), 2)  3.1 us
  transfers between devices with their start and end apart: 1, of which 1 were waited for; matrix products, arithmetic and copies ran while one was open for 5% of the time, Pallas kernels for 9%

profile of v4, /device:TPU:15, one launch (start us, length us, event | category | flops | bytes accessed | tf_op | source)
XLA Modules:
  0.0 151.4 jit_solution(3461634755877056234)
XLA Ops:
  0.6 0.0 copy-start
  0.6 0.8 convert_element_type.28
  1.4 1.0 slice_bitcast_fusion.31
  2.4 1.3 fusion.1
  3.8 0.1 slice_bitcast_fusion.7
  3.9 4.5 %select_select_fusion.hid_ref = bf16[16,128,384]{2,1,0:T(8,128)(2,1)} fusion(pred[16,128]{1,0:T(8,128)(4,1)S(1)} %get-tuple-element.66, pred[16,128]{1,0:T(8,128)(4,1)S(1)} %get-tuple-element.67, pred[16,128]{1,0:T(8,128)(4,1)S(1)} %get-tuple-element.68, pred[16,128]{1,0:T(8,128)(4,1)S(1)} %get-tuple-element.69, pred[16,128]{1,0:T(8,128)(4,1)S(1)} %get-tuple-element.70, ...), kind=kLoop, calls=%fused_computation.10 | loop fusion | flops 6291456 | bytes 2375680 | tf_op jit(solution)/shard_map/jit(_where)/select_n | solution.py:410
  8.4 74.1 %exchange.1 = (bf16[16,128,2048]{2,1,0:T(8,128)(2,1)}, bf16[16,128,384]{2,1,0:T(8,128)(2,1)}) custom-call(bf16[128,2048]{1,0:T(8,128)(2,1)} %grad_ref.1, bf16[16,128,384]{2,1,0:T(8,128)(2,1)} %select_select_fusion.hid_ref), custom_call_target="tpu_custom_call" | custom-call | tf_op jit(solution)/shard_map/exchange/pallas_call | solution.py:311
  82.5 0.0 copy-done
  82.5 9.2 %convolution_convert_fusion = bf16[2048,384]{1,0:T(8,128)(2,1)} fusion(bf16[2048,2048]{1,0:T(8,128)(2,1)} %bitcast.80, bf16[1,384,2048]{2,1,0:T(8,128)(2,1)S(1)} %copy-done), kind=kOutput, calls=%fused_computation.2 | convolution fusion | flops 3222011904 | bytes 11534336 | tf_op jit(solution)/shard_map/dot_general | solution.py:413
  91.6 0.0 copy-start.3
  91.6 17.1 %all-to-all-start = ((bf16[16,128,384]{2,1,0:T(8,128)(2,1)}), bf16[16,128,384]{2,1,0:T(8,128)(2,1)}, u32[]{:S(2)}, u32[]{:S(2)}) async-start(bf16[16,128,384]{2,1,0:T(8,128)(2,1)} %bitcast.22), calls=%async_computation | async-start | bytes 3145728 | tf_op jit(solution)/shard_map/all_to_all | solution.py:416
  108.7 0.0 copy-done.3
  108.8 7.8 %fusion = bf16[1,384,2048]{2,1,0:T(8,128)(2,1)S(1)} fusion(bf16[1,384,2048]{2,1,0:T(8,128)(2,1)} %param.11, bf16[16,128,384]{2,1,0:T(8,128)(2,1)} %get-tuple-element.8, bf16[16,128,2048]{2,1,0:T(8,128)(2,1)} %get-tuple-element.9), kind=kOutput, calls=%fused_computation.1 | convolution fusion | flops 3224371200 | bytes 13107200 | tf_op jit(solution)/shard_map/dot_general | solution.py:423
  116.6 0.0 copy-start.1
  116.6 13.3 %orthogonal.1 = f32[384,2048]{1,0:T(8,128)} custom-call(bf16[384,2048]{1,0:T(8,128)(2,1)S(1)} %bitcast.79), custom_call_target="tpu_custom_call" | custom-call | flops 6606028800 | bytes 4718592 | tf_op jit(solution)/shard_map/orthogonal/pallas_call | solution.py:381
  129.9 0.0 copy-done.1
  129.9 15.1 %all-to-all-done = bf16[16,128,384]{2,1,0:T(8,128)(2,1)} async-done(((bf16[16,128,384]{2,1,0:T(8,128)(2,1)}), bf16[16,128,384]{2,1,0:T(8,128)(2,1)}, u32[]{:S(2)}, u32[]{:S(2)}) %all-to-all-start) | async-done | bytes 1572896 | tf_op jit(solution)/shard_map/all_to_all | solution.py:416
  145.0 0.0 copy-start.2
  145.0 1.7 %slice_bitcast_fusion.23 = (bf16[128,384]{1,0:T(8,128)(2,1)S(1)}, bf16[128,384]{1,0:T(8,128)(2,1)S(1)}, bf16[128,384]{1,0:T(8,128)(2,1)S(1)}, bf16[128,384]{1,0:...) fusion(bf16[16,128,384]{2,1,0:T(8,128)(2,1)} %all-to-all-done), kind=kLoop, calls=%fused_computation.35 | loop fusion | bytes 3145728 | tf_op jit(solution)/shard_map/jit(_where)/broadcast_in_dim | solution.py:437
  146.7 0.0 copy-done.2
  146.7 3.1 %fusion.3 = (f32[128,8]{0,1:T(8,128)}, bf16[128,8,384]{2,0,1:T(8,128)(2,1)S(1)}) fusion(bf16[128,8,384]{2,1,0:T(8,128)(2,1)S(1)} %copy-done.2, bf16[128,384]{1,0:T(8,128)(2,1)S(1)} %get-tuple-element.19, pred[128,8]{0,1:T(8,128)(4,1)S(1)} %get-tuple-element.56, bf16[128,384]{1,0:T(8,128)(2,1)S(1)} %get-tuple-element.20, ...), kind=kLoop, calls=%fused_computation.8 | loop fusion | flops 7863296 | bytes 3166208 | tf_op jit(solution)/shard_map/reduce_sum | solution.py:441
  149.8 0.2 fusion.2
  150.0 1.3 copy.30
  (5 shorter events, 0.1 us)
Async XLA Ops:
  0.6 81.8 %copy-start = (bf16[1,384,2048]{2,1,0:T(8,128)(2,1)S(1)}, bf16[1,384,2048]{2,1,0:T(8,128)(2,1)}, u32[]{:S(2)}) copy-start(bf16[1,384,2048]{2,1,0:T(8,128)(2,1)} %param.10) | copy-start | bytes 4718596
  91.6 17.1 %copy-start.3 = (s32[128,8]{0,1:T(8,128)S(1)}, s32[128,8]{0,1:T(8,128)}, u32[]{:S(2)}) copy-start(s32[128,8]{0,1:T(8,128)} %param.7) | copy-start | bytes 12292
  91.6 53.3 %all-to-all-start = ((bf16[16,128,384]{2,1,0:T(8,128)(2,1)}), bf16[16,128,384]{2,1,0:T(8,128)(2,1)}, u32[]{:S(2)}, u32[]{:S(2)}) async-start(bf16[16,128,384]{2,1,0:T(8,128)(2,1)} %bitcast.22), calls=%async_computation | async-start | bytes 3145728 | tf_op jit(solution)/shard_map/all_to_all | solution.py:416
  116.6 13.3 %copy-start.1 = (bf16[1,384,2048]{2,1,0:T(8,128)(2,1)}, bf16[1,384,2048]{2,1,0:T(8,128)(2,1)S(1)}, u32[]{:S(2)}) copy-start(bf16[1,384,2048]{2,1,0:T(8,128)(2,1)S(1)} %fusion) | copy-start | bytes 4718596
  145.0 1.7 %copy-start.2 = (bf16[128,8,384]{2,1,0:T(8,128)(2,1)S(1)}, bf16[128,8,384]{2,1,0:T(8,128)(2,1)}, u32[]{:S(2)}) copy-start(bf16[128,8,384]{2,1,0:T(8,128)(2,1)} %param.9) | copy-start | bytes 2359300

commit v5 on v4

--- a/solution.py
+++ b/solution.py
@@ -124,8 +124,11 @@
     width,
     grad_ref,
     hid_ref,
+    weight_ref,
     all_ref,
     recv_ref,
+    raw_ref,
+    rows_ref,
     local_sem,
     up_sem,
     down_sem,
@@ -278,6 +281,18 @@
     def _(source_row):
         arrive(source_row, sibling)
         arrive(source_row, cross_sibling)
+        load = pltpu.make_async_copy(
+            all_ref.at[pl.ds(source_row * width, width)], rows_ref, local_sem.at[0]
+        )
+        load.start()
+        load.wait()
+        for place in range(width):
+            raw_ref[source_row * width + place] = lax.dot_general(
+                rows_ref[place],
+                weight_ref[...],
+                (((1,), (1,)), ((), ())),
+                preferred_element_type=jnp.float32,
+            ).astype(raw_ref.dtype)
         over(source_row).wait_send()
         aside(source_row, 0).wait_send()
         aside(source_row, 1).wait_send()
@@ -304,7 +319,7 @@
         ).wait_recv()
 
 
-def exchange(grad_out, send_hidden):
+def exchange(grad_out, send_hidden, weight):
     owners, width = lax.axis_size("expert"), lax.axis_size("dp")
     total = owners * width
     dma = pltpu.SemaphoreType.DMA
@@ -313,10 +328,13 @@
         out_shape=(
             jax.ShapeDtypeStruct((total,) + grad_out.shape, grad_out.dtype),
             jax.ShapeDtypeStruct(send_hidden.shape, send_hidden.dtype),
+            jax.ShapeDtypeStruct(send_hidden.shape, send_hidden.dtype),
         ),
-        in_specs=[pl.BlockSpec(memory_space=pl.ANY)] * 2,
-        out_specs=(pl.BlockSpec(memory_space=pl.ANY),) * 2,
+        in_specs=[pl.BlockSpec(memory_space=pl.ANY)] * 2 + [pl.BlockSpec(memory_space=pltpu.VMEM)],
+        out_specs=(pl.BlockSpec(memory_space=pl.ANY),) * 2
+        + (pl.BlockSpec(memory_space=pltpu.VMEM),),
         scratch_shapes=[
+            pltpu.VMEM((width,) + grad_out.shape, grad_out.dtype),
             dma((2,)),
             dma((owners,)),
             dma((owners,)),
@@ -326,9 +344,9 @@
             dma((total,)),
             dma((total,)),
         ],
-        compiler_params=pltpu.CompilerParams(collective_id=0, has_side_effects=True),
+        compiler_params=pltpu.CompilerParams(collective_id=0, has_side_effects=True, vmem_limit_bytes=24 * 2**20),
         name="exchange",
-    )(grad_out, send_hidden)
+    )(grad_out, send_hidden, weight)
 
 
 def orthogonal_kernel(tiles, momentum_ref, update_ref, iterate_ref):
@@ -408,13 +426,10 @@
     for choice in range(top_count):
         named = expert_ids[None, :, choice] == experts[:, None]
         send_hidden = jnp.where(named[..., None], prob_hidden[None, :, choice], send_hidden)
-    all_grad, recv_hidden = exchange(grad_out, send_hidden)
+    all_grad, recv_hidden, raw_grad = exchange(grad_out, send_hidden, weights[0])
     all_grad = all_grad.reshape(device_count * tok_rows, model_width)
-    raw_grad = lax.dot_general(
-        all_grad, weights[0], (((1,), (1,)), ((), ())), preferred_element_type=jnp.float32
-    ).astype(jnp.bfloat16)
     returned = lax.all_to_all(
-        raw_grad.reshape(device_count, tok_rows, hidden_width),
+        raw_grad,
         axes,
         split_axis=0,
         concat_axis=0,

time: 152 us -> 151 us (level)
  matrix products: 17 us -> 7.42 us
  Pallas kernels: 87.4 us -> 91.9 us
  local copies, waits for them, and re-layouts: 4.15 us -> 7.37 us
  starting transfers between devices: 17.1 us -> 19.7 us
  other arithmetic: 9.97 us -> 8.31 us
    dot_general x1 -> x0, matrix products: 9.16 us -> none  [dense_shards(): lax.dot_general(all_grad, weights[0], (((1,), (1,)), ((), ())), preferred...]
    pallas_call x1, Pallas kernels: 74.1 us -> 78.6 us  [exchange(): pl.pallas_call(functools.partial(exchange_kernel, owners, width), out_sha...]
    unnamed x9 -> x13, local copies, waits for them, and re-layouts: 1.36 us -> 4.58 us
    all_to_all x1, starting transfers between devices: 17.1 us -> 19.7 us  [dense_shards(): lax.all_to_all(raw_grad, axes, split_axis=0, concat_axis=0, tiled=True)]
    select_n x1, other arithmetic: 4.48 us -> 2.92 us  [dense_shards(): jnp.where(named[..., None], prob_hidden[None, :, choice], send_hidden)]
where the time goes in v5:
time: 151 us
  Pallas kernels  91.9 us (61%)
  starting transfers between devices  19.7 us (13%)
  waiting for transfers between devices  15.5 us (10%)
  other arithmetic  8.31 us (6%)
  matrix products  7.42 us (5%)
  local copies, waits for them, and re-layouts  7.37 us (5%)
    pallas_call x1, Pallas kernels, exchange(): pl.pallas_call(functools.partial(exchange_kernel, owners, width), out_sha...  78.6 us
    all_to_all x1, starting transfers between devices, dense_shards(): lax.all_to_all(raw_grad, axes, split_axis=0, concat_axis=0, tiled=True)  19.7 us
    all_to_all x1, waiting for transfers between devices, dense_shards(): lax.all_to_all(raw_grad, axes, split_axis=0, concat_axis=0, tiled=True)  15.5 us
    pallas_call x1, Pallas kernels, orthogonal_block(): pl.pallas_call(functools.partial(orthogonal_kernel, width // 512), out_sh...  13.3 us
    dot_general x1, matrix products, dense_shards(): lax.dot_general(recv_hidden.reshape(device_count * tok_rows, hidden_width...  7.42 us
    unnamed x13, local copies, waits for them, and re-layouts  4.58 us
    reduce_sum x1, other arithmetic, dense_shards(): jnp.sum(raw_rows.astype(jnp.float32) * hidden.astype(jnp.float32), 2)  3.12 us
  transfers between devices with their start and end apart: 1, of which 1 were waited for; matrix products, arithmetic and copies ran while one was open for 5% of the time, Pallas kernels for 9%

profile of v5, /device:TPU:15, one launch (start us, length us, event | category | flops | bytes accessed | tf_op | source)
XLA Modules:
  0.0 151.0 jit_solution(9295434936332564483)
XLA Ops:
  0.6 1.0 slice_bitcast_fusion.31
  1.6 0.7 convert_element_type.25
  2.3 1.3 fusion.1
  3.6 0.1 slice_bitcast_fusion.7
  3.7 0.0 copy-start
  3.8 0.0 copy-start.1
  3.8 2.9 %select_select_fusion.hid_ref = bf16[16,128,384]{2,1,0:T(8,128)(2,1)S(1)} fusion(pred[16,128]{1,0:T(8,128)(4,1)S(1)} %get-tuple-element.68, pred[16,128]{1,0:T(8,128)(4,1)S(1)} %get-tuple-element.69, pred[16,128]{1,0:T(8,128)(4,1)S(1)} %get-tuple-element.70, pred[16,128]{1,0:T(8,128)(4,1)S(1)} %get-tuple-element.71, ...), kind=kLoop, calls=%fused_computation.8 | loop fusion | flops 6291456 | bytes 2375680 | tf_op jit(solution)/shard_map/jit(_where)/select_n | solution.py:428
  6.7 0.0 copy-done
  6.8 0.0 copy-done.1
  6.8 78.6 %exchange.1 = (bf16[16,128,2048]{2,1,0:T(8,128)(2,1)S(1)}, bf16[16,128,384]{2,1,0:T(8,128)(2,1)S(1)}, bf16[16,128,384]{2,1,0:T(8,128)(2,1)}) custom-call(bf16[128,2048]{1,0:T(8,128)(2,1)S(1)} %copy-done.1, bf16[16,128,384]{2,1,0:T(8,128)(2,1)S(1)} %select_select_fusion.hid_ref, bf16[384,2048]{1,0:T(8,128)(2,1)S(1)} %bitcast.74), custom_call_target="tpu_custom_call" | custom-call | tf_op jit(solution)/shard_map/exchange/pallas_call | solution.py:326
  85.4 0.0 copy-start.2
  85.4 3.2 %copy-done.2 = bf16[16,128,2048]{2,1,0:T(8,128)(2,1)} copy-done((bf16[16,128,2048]{2,1,0:T(8,128)(2,1)}, bf16[16,128,2048]{2,1,0:T(8,128)(2,1)S(1)}, u32[]{:S(2)}) %copy-start.2) | copy-done | bytes 8388632
  88.6 19.7 %all-to-all-start = ((bf16[16,128,384]{2,1,0:T(8,128)(2,1)}), bf16[16,128,384]{2,1,0:T(8,128)(2,1)}, u32[]{:S(2)}, u32[]{:S(2)}) async-start(bf16[16,128,384]{2,1,0:T(8,128)(2,1)} %get-tuple-element.11), calls=%async_computation | async-start | bytes 3145728 | tf_op jit(solution)/shard_map/all_to_all | solution.py:431
  108.3 0.0 copy-done.5
  108.3 7.4 %fusion = bf16[1,384,2048]{2,1,0:T(8,128)(2,1)S(1)} fusion(bf16[1,384,2048]{2,1,0:T(8,128)(2,1)} %param.11, bf16[16,128,384]{2,1,0:T(8,128)(2,1)S(1)} %get-tuple-element.9, bf16[16,128,2048]{2,1,0:T(8,128)(2,1)} %copy-done.2), kind=kOutput, calls=%fused_computation.1 | convolution fusion | flops 3224371200 | bytes 13107200 | tf_op jit(solution)/shard_map/dot_general | solution.py:438
  115.8 0.0 copy-start.3
  115.8 13.3 %orthogonal.1 = f32[384,2048]{1,0:T(8,128)} custom-call(bf16[384,2048]{1,0:T(8,128)(2,1)S(1)} %bitcast.75), custom_call_target="tpu_custom_call" | custom-call | flops 6606028800 | bytes 4718592 | tf_op jit(solution)/shard_map/orthogonal/pallas_call | solution.py:399
  129.1 0.0 copy-done.3
  129.1 15.5 %all-to-all-done = bf16[16,128,384]{2,1,0:T(8,128)(2,1)} async-done(((bf16[16,128,384]{2,1,0:T(8,128)(2,1)}), bf16[16,128,384]{2,1,0:T(8,128)(2,1)}, u32[]{:S(2)}, u32[]{:S(2)}) %all-to-all-start) | async-done | bytes 1572896 | tf_op jit(solution)/shard_map/all_to_all | solution.py:431
  144.6 1.7 %slice_bitcast_fusion.23 = (bf16[128,384]{1,0:T(8,128)(2,1)S(1)}, bf16[128,384]{1,0:T(8,128)(2,1)S(1)}, bf16[128,384]{1,0:T(8,128)(2,1)S(1)}, bf16[128,384]{1,0:...) fusion(bf16[16,128,384]{2,1,0:T(8,128)(2,1)} %all-to-all-done), kind=kLoop, calls=%fused_computation.33 | loop fusion | bytes 3145728 | tf_op jit(solution)/shard_map/jit(_where)/broadcast_in_dim | solution.py:452
  146.3 0.0 copy-done.4
  146.4 3.1 %fusion.3 = (f32[128,8]{0,1:T(8,128)}, bf16[128,8,384]{2,0,1:T(8,128)(2,1)S(1)}) fusion(bf16[128,8,384]{2,1,0:T(8,128)(2,1)S(1)} %copy-done.4, bf16[128,384]{1,0:T(8,128)(2,1)S(1)} %get-tuple-element.21, pred[128,8]{0,1:T(8,128)(4,1)S(1)} %get-tuple-element.58, bf16[128,384]{1,0:T(8,128)(2,1)S(1)} %get-tuple-element.22, ...), kind=kLoop, calls=%fused_computation.7 | loop fusion | flops 7863296 | bytes 3166208 | tf_op jit(solution)/shard_map/reduce_sum | solution.py:456
  149.5 0.2 fusion.2
  149.7 1.3 copy.30
  (7 shorter events, 0.1 us)
Async XLA Ops:
  3.7 3.0 %copy-start = (bf16[1,384,2048]{2,1,0:T(8,128)(2,1)S(1)}, bf16[1,384,2048]{2,1,0:T(8,128)(2,1)}, u32[]{:S(2)}) copy-start(bf16[1,384,2048]{2,1,0:T(8,128)(2,1)} %param.10) | copy-start | bytes 4718596
  3.8 3.0 %copy-start.1 = (bf16[128,2048]{1,0:T(8,128)(2,1)S(1)}, bf16[128,2048]{1,0:T(8,128)(2,1)}, u32[]{:S(2)}) copy-start(bf16[128,2048]{1,0:T(8,128)(2,1)} %grad_ref.1) | copy-start | bytes 1572868
  85.4 3.2 %copy-start.2 = (bf16[16,128,2048]{2,1,0:T(8,128)(2,1)}, bf16[16,128,2048]{2,1,0:T(8,128)(2,1)S(1)}, u32[]{:S(2)}) copy-start(bf16[16,128,2048]{2,1,0:T(8,128)(2,1)S(1)} %get-tuple-element.10) | copy-start | bytes 25165828
  88.6 19.7 %copy-start.5 = (s32[128,8]{0,1:T(8,128)S(1)}, s32[128,8]{0,1:T(8,128)}, u32[]{:S(2)}) copy-start(s32[128,8]{0,1:T(8,128)} %param.7) | copy-start | bytes 12292
  88.6 56.0 %all-to-all-start = ((bf16[16,128,384]{2,1,0:T(8,128)(2,1)}), bf16[16,128,384]{2,1,0:T(8,128)(2,1)}, u32[]{:S(2)}, u32[]{:S(2)}) async-start(bf16[16,128,384]{2,1,0:T(8,128)(2,1)} %get-tuple-element.11), calls=%async_computation | async-start | bytes 3145728 | tf_op jit(solution)/shard_map/all_to_all | solution.py:431
  115.8 13.3 %copy-start.3 = (bf16[1,384,2048]{2,1,0:T(8,128)(2,1)}, bf16[1,384,2048]{2,1,0:T(8,128)(2,1)S(1)}, u32[]{:S(2)}) copy-start(bf16[1,384,2048]{2,1,0:T(8,128)(2,1)S(1)} %fusion) | copy-start | bytes 4718596
  144.6 1.7 %copy-start.4 = (bf16[128,8,384]{2,1,0:T(8,128)(2,1)S(1)}, bf16[128,8,384]{2,1,0:T(8,128)(2,1)}, u32[]{:S(2)}) copy-start(bf16[128,8,384]{2,1,0:T(8,128)(2,1)} %param.9) | copy-start | bytes 2359300
